TPU v7x, 32 devices: a whole 2x2x4 slice. The times are simulated.
32 devices in a mesh: slab: 16 (over z, y, x), coil: 2 (over core).
Axes of the slice: x: 2, y: 2, z: 4, core: 2. Of those that a mesh axis runs over, the one named last changes fastest.
Arguments:
- image: float32 [128, 2, 16, 384], P(('slab', 'coil')), may hold values from -6 to 6
- noise: float32 [128, 2, 16, 384], P(('slab', 'coil')), may hold values from -1.2 to 1.2
- sens: bfloat16 [16, 2, 16, 384, 128], P('coil', None, 'slab'), may hold values from -1 to 1
- measured: bfloat16 [16, 2, 16, 384, 128], P('coil', None, 'slab'), may hold values from -3 to 3
- mask: int32 [384, 128], replicated, may hold values 0 or 1
- w_first: bfloat16 [3, 3, 10, 128], replicated, may hold values from -0.625 to 0.625
- b_first: float32 [128], replicated, may hold values from -3 to 3
- w_second: bfloat16 [128, 128], replicated, may hold values from -0.5 to 0.5
- b_second: float32 [128], replicated, may hold values from -3 to 3
- w_third: bfloat16 [128, 128], replicated, may hold values from -0.5 to 0.5
- b_third: float32 [128], replicated, may hold values from -3 to 3
- w_last: bfloat16 [3, 3, 2, 128], replicated, may hold values from -0.1875 to 0.1875
Outputs:
- updated: float32 [128, 2, 16, 384], P(('slab', 'coil'))
Inputs may be any that keep to these rules, and one draw needn't show every extreme that they name: `mask`: 1 where the (ky, kz) line was measured, else 0.
All inputs are finite; a program needn't handle non-finite values.
Results may differ from a plain program's by a relative error of at most 0.0035.
Values may be sent and summed in bfloat16 or wider, within the bound.
No kernel may reach another device: no remote copies, remote signals or barrier semaphores. Data moves between devices by JAX's collectives and lax.ppermute only.
A program may use at most 256 MiB of HBM per device.

v0:
```python
import jax
import jax.numpy as jnp
import numpy as np
from jax import lax
from jax.experimental import pallas as pl
from jax.experimental.pallas import tpu as pltpu
from jax.sharding import PartitionSpec as P

STEP_SIZE = 0.5
F32 = jnp.float32
BF16 = jnp.bfloat16
QUAD = 4
GROUP = 8
VMEM_LIMIT = 24 * 2**20
BUSY = 4 * 10**10


def dot(lhs, rhs):
    return jnp.dot(lhs, rhs, preferred_element_type=F32)


def dot_tn(lhs, rhs):
    return lax.dot_general(lhs, rhs, (((0,), (0,)), ((), ())), preferred_element_type=F32)


def dot_nt(lhs, rhs):
    return lax.dot_general(lhs, rhs, (((1,), (1,)), ((), ())), preferred_element_type=F32)


def dft_table(length):
    index = np.arange(length)
    turns = (index[:, None] * index[None, :]) % length
    angle = turns * (2.0 * np.pi / length)
    scale = 1.0 / np.sqrt(length)
    cos = np.cos(angle) * scale
    sin = np.sin(angle) * scale
    return np.block([[cos, sin], [-sin, cos]]).astype(np.float32).astype(BF16)


def send_order(slices, rows):
    place = np.zeros((rows * slices * 2, slices * 2 * rows), np.float32)
    for z in range(slices):
        for p in range(2):
            for x in range(rows):
                place[(x * slices + z) * 2 + p, (z * 2 + p) * rows + x] = 1
    return place.astype(BF16)


def depth_order(devices, x_local, slices):
    depth = devices * slices
    place = np.zeros((x_local, devices * x_local * slices * 2, 2 * depth), np.float32)
    for d in range(devices):
        for x in range(x_local):
            for z in range(slices):
                for p in range(2):
                    place[x, ((d * x_local + x) * slices + z) * 2 + p, p * depth + d * slices + z] = 1
    return place.reshape(-1, 2 * depth).astype(BF16)


def gather_order(slabs, coils, x_local, slices):
    rows = slabs * x_local
    place = np.zeros((slices * 2 * rows, slabs * coils * x_local * slices * 2), np.float32)
    for s in range(slabs):
        for c in range(coils):
            for x in range(x_local):
                for z in range(slices):
                    for p in range(2):
                        source = (((s * coils + c) * x_local + x) * slices + z) * 2 + p
                        place[(z * 2 + p) * rows + s * x_local + x, source] = 1
    return place.astype(BF16)


def first_order():
    place = np.zeros((3, 5, 2, 8, QUAD, 5, 3, 2, GROUP), np.float32)
    for xo in range(QUAD):
        for a in range(3):
            for b in range(3):
                for o in range(5):
                    for p in range(2):
                        place[a, o, p, b, xo, o, b, p, xo + 1 + a] = 0.5
    return place.reshape(240, QUAD * 240).astype(BF16)


def last_order():
    place = np.zeros((QUAD, 3, 2, GROUP, 3, 3, 8), np.float32)
    for xo in range(QUAD):
        for j in range(GROUP):
            a = xo - j + 3
            if 0 <= a < 3:
                for b in range(3):
                    for o in range(2):
                        place[xo, b, o, j, a, b, o] = 1
    return place.reshape(QUAD * 48, 72).astype(BF16)


HBM = pl.BlockSpec(memory_space=pltpu.HBM)
VMEM = pl.BlockSpec(memory_space=pltpu.VMEM)


def fetch(sources, targets, sems):
    copies = [pltpu.make_async_copy(s, t, sems.at[i]) for i, (s, t) in enumerate(zip(sources, targets))]
    for copy in copies:
        copy.start()
    return copies


def room(*arrays):
    return [pltpu.VMEM(a.shape, a.dtype) for a in arrays] + [pltpu.SemaphoreType.DMA((len(arrays),))]


def call(kernel, out_shape, scratch=(), flops=0, nbytes=0, **kwargs):
    return pl.pallas_call(
        kernel,
        out_shape=out_shape,
        scratch_shapes=list(scratch),
        compiler_params=pltpu.CompilerParams(vmem_limit_bytes=VMEM_LIMIT),
        cost_estimate=pl.CostEstimate(flops=flops, bytes_accessed=nbytes, transcendentals=0),
        **kwargs,
    )


def pack_kernel(image_hbm, order_hbm, blocks_ref, low_ref, high_ref, image_ref, order_ref, sems):
    for copy in fetch((image_hbm, order_hbm), (image_ref, order_ref), sems):
        copy.wait()
    slices, parts, rows, cols = image_ref.shape
    copies = blocks_ref.shape[0] * blocks_ref.shape[1] // (slices * parts * rows)
    image = image_ref[...].astype(BF16)
    moved = dot(order_ref[...], image.reshape(slices * parts * rows, cols))
    slabs = blocks_ref.shape[0] // copies
    moved = moved.reshape(slabs, 1, blocks_ref.shape[1], cols)
    moved = jnp.broadcast_to(moved, (slabs, copies) + moved.shape[2:])
    blocks_ref[...] = moved.reshape(blocks_ref.shape).astype(BF16)
    even = lax.axis_index("coil") % 2 == 0
    first = image_ref[:2]
    last = image_ref[slices - 2 :]
    low_ref[...] = jnp.where(even, last, first).astype(BF16)
    high_ref[...] = jnp.where(even, first, last).astype(BF16)


def fold_weights(sources, targets, rows):
    first_order_ref, last_order_ref, first_ref, b1_ref, second_ref, b2_ref, third_ref, b3_ref, last_ref = sources
    w1_ref, c1_ref, w2_ref, c2_ref, w3_ref, c3_ref, w4_ref = targets
    width = second_ref.shape[0]

    def padded(ref):
        rows[...] = jnp.zeros_like(rows)
        outer, inner, count, _ = ref.shape
        for i in range(outer):
            for j in range(inner):
                rows[i * inner + j, :count] = ref[i, j].astype(F32)
        return rows[: outer * inner].reshape(outer * inner * 8, width).astype(BF16)

    placed = dot_tn(padded(first_ref), first_order_ref[...])
    for xo in range(QUAD):
        w1_ref[xo * width : (xo + 1) * width] = placed[:, xo * 240 : (xo + 1) * 240].astype(BF16)
    placed = dot(last_order_ref[...], padded(last_ref)).astype(BF16)
    for xo in range(QUAD):
        w4_ref[:, xo * width : (xo + 1) * width] = placed[xo * 48 : (xo + 1) * 48]
    for source, target in ((second_ref, w2_ref), (third_ref, w3_ref)):
        turned = (jnp.transpose(source[...].astype(F32)) * 0.5).astype(BF16)
        zeros = jnp.zeros_like(turned)
        target[...] = jnp.concatenate(
            [jnp.concatenate([turned, zeros], axis=1), jnp.concatenate([zeros, turned], axis=1)], axis=0
        )
    for source, target in ((b1_ref, c1_ref), (b2_ref, c2_ref), (b3_ref, c3_ref)):
        target[...] = jnp.transpose(jnp.broadcast_to(source[...] * 0.5, (width, width)))


def staggered(chains):
    waiting, running = list(chains), []
    while waiting or running:
        if waiting:
            running.append(waiting.pop(0))
        for one in running[::-1]:
            if next(one, one) is one:
                running.remove(one)


def half_silu(half):
    return (half + half * jnp.tanh(half)).astype(BF16)


def score_kernel(z_from, z_count, sources, n_ordered, *refs):
    refs, out_ref, scratch = refs[:sources], refs[sources + n_ordered], refs[sources + n_ordered + 1 :]
    folded, rows, scratch = scratch[:7], scratch[7], scratch[8:]
    fold_weights(refs[3:], folded, rows)
    score_slices(z_from, z_count, refs[:3], folded, out_ref, *scratch)


def score_slices(z_from, z_count, planes, weights, out_ref, shifted, windows, sums):
    image_ref, low_ref, high_ref = planes
    w1_ref, c1_ref, w2_ref, c2_ref, w3_ref, c3_ref, w4_ref = weights
    slices, _, rows, cols = image_ref.shape
    quads = rows // QUAD
    width = c1_ref.shape[0]
    even = lax.axis_index("coil") % 2 == 0

    def plane(z, p):
        if 0 <= z < slices:
            return image_ref[z, p].astype(BF16).astype(F32)
        i = z + 2 if z < 0 else z - slices
        one, two = low_ref[i, p].astype(F32), high_ref[i, p].astype(F32)
        return jnp.where(even, two, one) if z < 0 else jnp.where(even, one, two)

    def earlier(values):
        at = lax.broadcasted_iota(jnp.int32, values.shape, 1)
        return jnp.where(at == 0, 0.0, pltpu.roll(values, 1, 1))

    def later(values):
        at = lax.broadcasted_iota(jnp.int32, values.shape, 1)
        return jnp.where(at == cols - 1, 0.0, pltpu.roll(values, cols - 1, 1))

    shifted[...] = jnp.zeros_like(shifted)
    for i in range(z_count + 4):
        for p in range(2):
            values = plane(z_from + i - 2, p)
            for b, moved in enumerate((earlier(values), values, later(values))):
                shifted[b, 4 : 4 + rows] = moved
                for q in range(quads):
                    start = QUAD * q + 2
                    windows[q, i, b, p * GROUP : (p + 1) * GROUP] = shifted[b, start : start + GROUP].astype(BF16)

    spots = [(q, z) for z in range(z_count) for q in range(quads)]
    inputs = jnp.concatenate([windows[q, z : z + 5].reshape(240, cols) for q, z in spots], axis=1)
    pairs = {}

    def bias(ref, lanes):
        return jnp.concatenate([jnp.concatenate([ref[...]] * (lanes // 128), axis=1)] * 2, axis=0)

    def chain(start, stop, pair):
        half = slice(2 * width * pair, 2 * width * (pair + 1))
        lanes = stop - start
        total = dot(w1_ref[half], inputs[:, start:stop])
        yield
        hidden = half_silu(total + bias(c1_ref, lanes))
        yield
        total = dot(w2_ref[...], hidden)
        yield
        hidden = half_silu(total + bias(c2_ref, lanes))
        yield
        total = dot(w3_ref[...], hidden)
        yield
        hidden = half_silu(total + bias(c3_ref, lanes))
        yield
        pairs[start, pair] = dot(w4_ref[:, half], hidden)

    length = len(spots) * cols
    tile = 256
    staggered([chain(n, min(n + tile, length), pair) for n in range(0, length, tile) for pair in range(QUAD // 2)])
    taps = jnp.concatenate(
        [sum(pairs[n, pair] for pair in range(QUAD // 2)) for n in range(0, length, tile)], axis=1
    )
    for i, (q, z) in enumerate(spots):
        part = taps[:, i * cols : (i + 1) * cols]
        total = part[16:32] + earlier(part[:16]) + later(part[32:])
        sums[z, q, 0] = total[:GROUP]
        sums[z, q, 1] = total[GROUP:]
    for z in range(z_count):
        for o in range(2):
            shifted[0] = jnp.zeros_like(shifted[0])
            for q in range(quads):
                start = QUAD * q + 2
                shifted[0, start : start + GROUP] += sums[z, q, o]
            out_ref[z, o] = shifted[0, 4 : 4 + rows]


def adjoint_kernel(
    planes_ref, sens_ref, measured_ref, mask_ref, half_ref, z_ref, out_ref, y_ref
):
    blocks, block_rows, cols = planes_ref.shape
    coils, _, x_local, _, depth = sens_ref.shape
    y_ref[:cols] = half_ref[...]
    y_ref[cols:, :cols] = -half_ref[:, cols:]
    y_ref[cols:, cols:] = half_ref[:, :cols]
    received = planes_ref[...].astype(F32).reshape(blocks * block_rows, cols).astype(BF16)
    z_table = z_ref[: 2 * depth]
    per = max(1, 512 // depth)
    result = None
    for x in range(x_local):
        place = z_ref[2 * depth + x * blocks * block_rows : 2 * depth + (x + 1) * blocks * block_rows]
        planes = dot_tn(received, place)
        image_real = planes[:, :depth]
        image_imag = planes[:, depth:]
        totals = []

        def along_z(half, count):
            for i in range(count):
                at = slice(i * depth, (i + 1) * depth)
                yield dot(jnp.concatenate([half[:cols, at], half[cols:, at]], axis=1), z_table)

        def stack(top, bottom):
            return jnp.concatenate([jnp.concatenate(top, axis=1), jnp.concatenate(bottom, axis=1)], axis=0)

        def chain(group):
            reals, imags = [], []
            for c in group:
                sens_real = sens_ref[c, 0, x].astype(F32)
                sens_imag = sens_ref[c, 1, x].astype(F32)
                reals.append((sens_real * image_real - sens_imag * image_imag).astype(BF16))
                imags.append((sens_real * image_imag + sens_imag * image_real).astype(BF16))
            stacked = stack(reals, imags)
            yield
            half = dot(y_ref[...], stacked).astype(BF16)
            yield
            specs = list(along_z(half, len(group)))
            yield
            reals, imags = [], []
            for spec, c in zip(specs, group):
                sampled = mask_ref[...].astype(F32)
                reals.append((sampled * (spec[:, :depth] - measured_ref[c, 0, x].astype(F32))).astype(BF16))
                imags.append((sampled * (spec[:, depth:] - measured_ref[c, 1, x].astype(F32))).astype(BF16))
            stacked = stack(imags, reals)
            yield
            half = dot(y_ref[...], stacked).astype(BF16)
            yield
            backs = list(along_z(half, len(group)))
            yield
            for back, c in zip(backs, group):
                back_imag = back[:, :depth]
                back_real = back[:, depth:]
                sens_real = sens_ref[c, 0, x].astype(F32)
                sens_imag = sens_ref[c, 1, x].astype(F32)
                real = sens_real * back_real + sens_imag * back_imag
                imag = sens_real * back_imag - sens_imag * back_real
                if totals:
                    real, imag = totals[0] + real, totals[1] + imag
                totals[:] = [real, imag]

        staggered([chain(range(c, min(c + per, coils))) for c in range(0, coils, per)])
        total = jnp.concatenate(totals, axis=1).astype(BF16)
        placed = dot_nt(place, total)
        result = placed if result is None else result + placed
    out_ref[...] = result.reshape(out_ref.shape).astype(BF16)


def final_kernel(image_ref, noise_ref, one_ref, two_ref, back_ref, order_ref, out_ref):
    blocks, block_rows, cols = back_ref.shape
    received = back_ref[...].astype(F32).reshape(blocks * block_rows, cols).astype(BF16)
    gradient = dot(order_ref[...], received).reshape(image_ref.shape)
    cut = one_ref.shape[0]
    out_ref[:cut] = image_ref[:cut] + STEP_SIZE * (one_ref[...] - gradient[:cut]) + noise_ref[:cut]
    out_ref[cut:] = image_ref[cut:] + STEP_SIZE * (two_ref[...] - gradient[cut:]) + noise_ref[cut:]


def on_device(
    image, noise, sens, measured, mask, w_first, b_first, w_second, b_second, w_third, b_third, w_last
):
    slabs = lax.axis_size("slab")
    groups = lax.axis_size("coil")
    devices = slabs * groups
    slices, _, rows, cols = image.shape
    x_local = rows // slabs
    width = w_second.shape[0]
    depth = sens.shape[4]
    both = ("slab", "coil")
    block = jax.ShapeDtypeStruct((devices, x_local * slices * 2, cols), BF16)
    halo = jax.ShapeDtypeStruct((2, 2, rows, cols), BF16)

    order = jnp.asarray(send_order(slices, rows))
    blocks, low, high = call(
        pack_kernel, (block, halo, halo), room(image, order), flops=BUSY, nbytes=10**6, in_specs=[HBM] * 2
    )(image, order)
    pairs = [(i, i ^ 1) for i in range(devices)]
    across = [(i, ((i + 1) ^ 1) - 1) for i in range(1, devices - 1)]
    low = lax.ppermute(low, both, pairs)
    high = lax.ppermute(high, both, across)
    planes = lax.all_to_all(blocks, both, split_axis=0, concat_axis=0, tiled=True)

    cut = slices // 2
    sources = (
        image, low, high, jnp.asarray(first_order()), jnp.asarray(last_order()),
        jnp.transpose(w_first, (0, 2, 1, 3)), b_first[None],
        w_second, b_second[None], w_third, b_third[None], w_last,
    )

    def score(z_from, count, *ordered):
        return call(
            lambda *refs: score_kernel(z_from, count, len(sources), len(ordered), *refs),
            jax.ShapeDtypeStruct((count, 2, rows, cols), F32),
            [
                pltpu.VMEM((QUAD * width, 240), BF16),
                pltpu.VMEM((width, width), F32),
                pltpu.VMEM((2 * width, 2 * width), BF16),
                pltpu.VMEM((width, width), F32),
                pltpu.VMEM((2 * width, 2 * width), BF16),
                pltpu.VMEM((width, width), F32),
                pltpu.VMEM((48, QUAD * width), BF16),
                pltpu.VMEM((30, 8, width), F32),
                pltpu.VMEM((3, rows + 8, cols), F32),
                pltpu.VMEM((rows // QUAD, count + 4, 3, 2 * GROUP, cols), BF16),
                pltpu.VMEM((count, rows // QUAD, 2, GROUP, cols), F32),
            ],
            flops=BUSY,
            nbytes=2 * 10**6,
            in_specs=[VMEM] * len(sources) + [pl.BlockSpec(memory_space=pl.ANY)] * len(ordered),
        )(*sources, *ordered)

    score_one = score(0, cut)
    z_tables = np.concatenate([dft_table(depth).T, depth_order(devices, x_local, slices)], axis=0)
    partial = call(
        adjoint_kernel, block, [pltpu.VMEM((2 * cols, 2 * cols), BF16)], flops=BUSY, nbytes=5 * 10**6, in_specs=[VMEM] * 6
    )(planes, sens, measured, mask, jnp.asarray(dft_table(cols)[:cols]), jnp.asarray(z_tables))
    score_two = score(cut, slices - cut, partial)
    back = lax.all_to_all(partial, both, split_axis=0, concat_axis=0, tiled=True)
    return call(final_kernel, jax.ShapeDtypeStruct(image.shape, F32), nbytes=10**6)(
        image, noise, score_one, score_two, back,
        jnp.asarray(gather_order(slabs, groups, x_local, slices)),
    )


def solution(mesh):
    whole = P(("slab", "coil"), None, None, None)
    by_coil = P("coil", None, "slab", None, None)
    return jax.shard_map(
        on_device,
        mesh=mesh,
        in_specs=(whole, whole, by_coil, by_coil) + (P(),) * 8,
        out_specs=whole,
        check_vma=False,
    )
```

profile of v0, /device:TPU:1, one launch (start us, length us, event | category | flops | bytes accessed | tf_op | source)
XLA Modules:
  0.0 40.8 jit_solution(2762177688284487462)
XLA Ops:
  0.0 0.9 %copy-done = f32[4,2,16,384]{3,2,1,0:T(8,128)S(1)} copy-done((f32[4,2,16,384]{3,2,1,0:T(8,128)S(1)}, f32[4,2,16,384]{3,2,1,0:T(8,128)}, u32[]{:S(2)}) %copy-start) | copy-done | bytes 196632
  0.9 0.8 %copy-done.19 = bf16[128,128]{1,0:T(8,128)(2,1)S(1)} copy-done((bf16[128,128]{1,0:T(8,128)(2,1)S(1)}, bf16[128,128]{1,0:T(8,128)(2,1)}, u32[]{:S(2)}) %copy-start.19) | copy-done | bytes 32792
  1.7 0.0 copy-start.18
  1.8 1.2 %shard_map.172 = (bf16[32,8,384]{2,1,0:T(8,128)(2,1)}, bf16[2,2,16,384]{3,2,1,0:T(8,128)(2,1)S(1)}, bf16[2,2,16,384]{3,2,1,0:T(8,128)(2,1)S(1)}) custom-call(f32[4,2,16,384]{3,2,1,0:T(8,128)S(1)} %copy-done, bf16[128,128]{1,0:T(8,128)(2,1)S(1)} %copy-done.19), custom_call_target="tpu_custom_call" | custom-call | flops 40000000000 | bytes 1000000 | tf_op jit(solution)/shard_map/pallas_call | solution.py:360
  2.9 0.1 collective-permute-start
  3.0 4.5 %collective-permute-start.1 = (bf16[2,2,16,384]{3,2,1,0:T(8,128)(2,1)S(1)}, bf16[2,2,16,384]{3,2,1,0:T(8,128)(2,1)S(1)}, u32[]{:S(2)}, u32[]{:S(2)}) collective-permute-start(bf16[2,2,16,384]{3,2,1,0:T(8,128)(2,1)S(1)} %get-tuple-element.9), channel_id=1, source_target_pairs={{1,2},{2,1},{3,4},{4,3},{5,6},{6,5},{7,8},{8,7},{9,10},{10,9},{11,... | collective-permute-start | bytes 147464 | tf_op jit(solution)/shard_map/ppermute | solution.py:366
  7.5 5.1 %all-to-all-start = ((bf16[32,8,384]{2,1,0:T(8,128)(2,1)}), bf16[32,8,384]{2,1,0:T(8,128)(2,1)S(1)}, u32[]{:S(2)}, u32[]{:S(2)}) async-start(bf16[32,8,384]{2,1,0:T(8,128)(2,1)} %get-tuple-element.10), calls=%async_computation | async-start | bytes 393216 | tf_op jit(solution)/shard_map/all_to_all | solution.py:367
  12.7 0.0 collective-permute-done.refs_1_
  12.7 0.0 collective-permute-done.1.refs_2_
  12.7 0.0 copy-done.1
  12.7 0.0 copy-done.7
  12.8 0.0 copy-start.15
  12.8 1.0 %copy-done.15 = bf16[240,960]{1,0:T(8,128)(2,1)S(1)} copy-done((bf16[240,960]{1,0:T(8,128)(2,1)S(1)}, bf16[240,960]{1,0:T(8,128)(2,1)}, u32[]{:S(2)}) %copy-start.15) | copy-done | bytes 460824
  13.8 4.7 %shard_map.173.one_ref = f32[2,2,16,384]{3,2,1,0:T(8,128)S(1)} custom-call(f32[4,2,16,384]{3,2,1,0:T(8,128)S(1)} %copy-done.1, bf16[2,2,16,384]{3,2,1,0:T(8,128)(2,1)S(1)} %collective-permute-done.refs_1_, bf16[2,2,16,384]{3,2,1,0:T(8,128)(2,1)S(1)} %collective-permute-done.1.refs_2_, bf16[240,960]{1,0:T(8,128)(2,1)S(1)} %copy-done.15, ...), custom_call_target="tpu_custom_call" | custom-call | flops 40000000000 | bytes 2000000 | tf_op jit(solution)/shard_map/pallas_call | solution.py:377
  18.5 3.4 %all-to-all-done.planes_ref = bf16[32,8,384]{2,1,0:T(8,128)(2,1)S(1)} async-done(((bf16[32,8,384]{2,1,0:T(8,128)(2,1)}), bf16[32,8,384]{2,1,0:T(8,128)(2,1)S(1)}, u32[]{:S(2)}, u32[]{:S(2)}) %all-to-all-start) | async-done | bytes 196640 | tf_op jit(solution)/shard_map/all_to_all | solution.py:367
  21.9 0.0 copy-start.5
  21.9 1.4 %copy-done.5 = bf16[8,2,1,384,128]{4,3,2,1,0:T(8,128)(2,1)S(1)} copy-done((bf16[8,2,1,384,128]{4,3,2,1,0:T(8,128)(2,1)S(1)}, bf16[8,2,1,384,128]{4,3,2,1,0:T(8,128)(2,1)}, u32[]{:S(2)}) %copy-start.5) | copy-done | bytes 1572888
  23.3 4.9 %shard_map.174.refs_12_ = bf16[32,8,384]{2,1,0:T(8,128)(2,1)} custom-call(bf16[32,8,384]{2,1,0:T(8,128)(2,1)S(1)} %all-to-all-done.planes_ref, bf16[8,2,1,384,128]{4,3,2,1,0:T(8,128)(2,1)S(1)} %copy-done.4, bf16[8,2,1,384,128]{4,3,2,1,0:T(8,128)(2,1)S(1)} %copy-done.5, s32[384,128]{1,0:T(8,128)S(1)} %copy-done.6, bf16[384,768]{1,0:T(8,128)(2,1)S(1)} %copy-done.14, ...), custom_call_target="tpu_custom_call" | custom-call | flops 40000000000 | bytes 5000000 | tf_op jit(solution)/shard_map/pallas_call | solution.py:400
  28.2 2.5 %all-to-all-start.1 = ((bf16[32,8,384]{2,1,0:T(8,128)(2,1)}), bf16[32,8,384]{2,1,0:T(8,128)(2,1)S(1)}, u32[]{:S(2)}, u32[]{:S(2)}) async-start(bf16[32,8,384]{2,1,0:T(8,128)(2,1)} %shard_map.174.refs_12_), calls=%async_computation.1 | async-start | bytes 393216 | tf_op jit(solution)/shard_map/all_to_all | solution.py:404
  30.7 0.0 copy-start.16
  30.7 1.0 %copy-done.16 = bf16[240,960]{1,0:T(8,128)(2,1)S(1)} copy-done((bf16[240,960]{1,0:T(8,128)(2,1)S(1)}, bf16[240,960]{1,0:T(8,128)(2,1)}, u32[]{:S(2)}) %copy-start.16) | copy-done | bytes 460824
  31.7 4.7 %shard_map.175.two_ref = f32[2,2,16,384]{3,2,1,0:T(8,128)S(1)} custom-call(f32[4,2,16,384]{3,2,1,0:T(8,128)S(1)} %copy-done.1, bf16[2,2,16,384]{3,2,1,0:T(8,128)(2,1)S(1)} %collective-permute-done.refs_1_, bf16[2,2,16,384]{3,2,1,0:T(8,128)(2,1)S(1)} %collective-permute-done.1.refs_2_, bf16[240,960]{1,0:T(8,128)(2,1)S(1)} %copy-done.16, ...), custom_call_target="tpu_custom_call" | custom-call | flops 40000000000 | bytes 2000000 | tf_op jit(solution)/shard_map/pallas_call | solution.py:377
  36.4 3.5 %all-to-all-done.1.back_ref = bf16[32,8,384]{2,1,0:T(8,128)(2,1)S(1)} async-done(((bf16[32,8,384]{2,1,0:T(8,128)(2,1)}), bf16[32,8,384]{2,1,0:T(8,128)(2,1)S(1)}, u32[]{:S(2)}, u32[]{:S(2)}) %all-to-all-start.1) | async-done | bytes 196640 | tf_op jit(solution)/shard_map/all_to_all | solution.py:404
  39.9 0.9 %shard_map.176 = f32[4,2,16,384]{3,2,1,0:T(8,128)} custom-call(f32[4,2,16,384]{3,2,1,0:T(8,128)S(1)} %copy-done.1, f32[4,2,16,384]{3,2,1,0:T(8,128)S(1)} %copy-done.2, f32[2,2,16,384]{3,2,1,0:T(8,128)S(1)} %shard_map.173.one_ref, f32[2,2,16,384]{3,2,1,0:T(8,128)S(1)} %shard_map.175.two_ref, bf16[32,8,384]{2,1,0:T(8,128)(2,1)S(1)} %all-to-all-done.1.back_ref, ...), custom_call_target="tpu_custom_call" | custom-call | bytes 1000000 | tf_op jit(solution)/shard_map/pallas_call | solution.py:405
  (29 shorter events, 0.1 us)
Async XLA Ops:
  0.0 0.9 %copy-start = (f32[4,2,16,384]{3,2,1,0:T(8,128)S(1)}, f32[4,2,16,384]{3,2,1,0:T(8,128)}, u32[]{:S(2)}) copy-start(f32[4,2,16,384]{3,2,1,0:T(8,128)} %image_ref.1) | copy-start | bytes 589828
  0.9 0.8 %copy-start.19 = (bf16[128,128]{1,0:T(8,128)(2,1)S(1)}, bf16[128,128]{1,0:T(8,128)(2,1)}, u32[]{:S(2)}) copy-start(bf16[128,128]{1,0:T(8,128)(2,1)} %constant.12.clone.order_hbm) | copy-start | bytes 98308
  1.7 11.0 %copy-start.1 = (f32[4,2,16,384]{3,2,1,0:T(8,128)S(1)}, f32[4,2,16,384]{3,2,1,0:T(8,128)}, u32[]{:S(2)}) copy-start(f32[4,2,16,384]{3,2,1,0:T(8,128)} %image_ref.1) | copy-start | bytes 589828
  1.7 11.0 %copy-start.7 = (bf16[128,128]{1,0:T(8,128)(2,1)S(1)}, bf16[128,128]{1,0:T(8,128)(2,1)}, u32[]{:S(2)}) copy-start(bf16[128,128]{1,0:T(8,128)(2,1)} %refs_7_.3) | copy-start | bytes 98308
  1.7 11.0 %copy-start.8 = (bf16[128,128]{1,0:T(8,128)(2,1)S(1)}, bf16[128,128]{1,0:T(8,128)(2,1)}, u32[]{:S(2)}) copy-start(bf16[128,128]{1,0:T(8,128)(2,1)} %refs_9_.3) | copy-start | bytes 98308
  1.7 11.0 %copy-start.9 = (bf16[3,3,10,128]{3,1,2,0:T(4,128)(2,1)S(1)}, bf16[3,3,10,128]{3,1,2,0:T(4,128)(2,1)}, u32[]{:S(2)}) copy-start(bf16[3,3,10,128]{3,1,2,0:T(4,128)(2,1)} %param.23) | copy-start | bytes 69124
  1.7 11.0 %copy-start.10 = (bf16[3,3,2,128]{3,2,1,0:T(2,128)(2,1)S(1)}, bf16[3,3,2,128]{3,2,1,0:T(2,128)(2,1)}, u32[]{:S(2)}) copy-start(bf16[3,3,2,128]{3,2,1,0:T(2,128)(2,1)} %refs_11_.3) | copy-start | bytes 13828
  1.7 11.0 %copy-start.11 = (f32[128]{0:T(128)S(1)}, f32[128]{0:T(128)}, u32[]{:S(2)}) copy-start(f32[128]{0:T(128)} %param.24) | copy-start | bytes 1540
  1.7 11.0 %copy-start.12 = (f32[128]{0:T(128)S(1)}, f32[128]{0:T(128)}, u32[]{:S(2)}) copy-start(f32[128]{0:T(128)} %param.26) | copy-start | bytes 1540
  1.7 11.0 %copy-start.13 = (f32[128]{0:T(128)S(1)}, f32[128]{0:T(128)}, u32[]{:S(2)}) copy-start(f32[128]{0:T(128)} %param.28) | copy-start | bytes 1540
  1.7 11.0 %copy-start.18 = (bf16[192,72]{1,0:T(8,128)(2,1)S(1)}, bf16[192,72]{1,0:T(8,128)(2,1)}, u32[]{:S(2)}) copy-start(bf16[192,72]{1,0:T(8,128)(2,1)} %constant.14.clone.refs_4_) | copy-start | bytes 82948
  2.9 9.7 %collective-permute-start = (bf16[2,2,16,384]{3,2,1,0:T(8,128)(2,1)S(1)}, bf16[2,2,16,384]{3,2,1,0:T(8,128)(2,1)S(1)}, u32[]{:S(2)}, u32[]{:S(2)}) collective-permute-start(bf16[2,2,16,384]{3,2,1,0:T(8,128)(2,1)S(1)} %get-tuple-element.8), channel_id=1, source_target_pairs={{0,1},{1,0},{2,3},{3,2},{4,5},{5,4},{6,7},{7,6},{8,9},{9,8},{10,11... | collective-permute-start | bytes 147464 | tf_op jit(solution)/shard_map/ppermute | solution.py:365
  3.0 9.6 %collective-permute-start.1 = (bf16[2,2,16,384]{3,2,1,0:T(8,128)(2,1)S(1)}, bf16[2,2,16,384]{3,2,1,0:T(8,128)(2,1)S(1)}, u32[]{:S(2)}, u32[]{:S(2)}) collective-permute-start(bf16[2,2,16,384]{3,2,1,0:T(8,128)(2,1)S(1)} %get-tuple-element.9), channel_id=1, source_target_pairs={{1,2},{2,1},{3,4},{4,3},{5,6},{6,5},{7,8},{8,7},{9,10},{10,9},{11,... | collective-permute-start | bytes 147464 | tf_op jit(solution)/shard_map/ppermute | solution.py:366
  7.5 14.4 %all-to-all-start = ((bf16[32,8,384]{2,1,0:T(8,128)(2,1)}), bf16[32,8,384]{2,1,0:T(8,128)(2,1)S(1)}, u32[]{:S(2)}, u32[]{:S(2)}) async-start(bf16[32,8,384]{2,1,0:T(8,128)(2,1)} %get-tuple-element.10), calls=%async_computation | async-start | bytes 393216 | tf_op jit(solution)/shard_map/all_to_all | solution.py:367
  12.8 1.0 %copy-start.15 = (bf16[240,960]{1,0:T(8,128)(2,1)S(1)}, bf16[240,960]{1,0:T(8,128)(2,1)}, u32[]{:S(2)}) copy-start(bf16[240,960]{1,0:T(8,128)(2,1)} %constant.13.clone.refs_3_) | copy-start | bytes 1382404
  13.8 8.1 %copy-start.4 = (bf16[8,2,1,384,128]{4,3,2,1,0:T(8,128)(2,1)S(1)}, bf16[8,2,1,384,128]{4,3,2,1,0:T(8,128)(2,1)}, u32[]{:S(2)}) copy-start(bf16[8,2,1,384,128]{4,3,2,1,0:T(8,128)(2,1)} %sens_ref.1) | copy-start | bytes 4718596
  13.8 8.1 %copy-start.6 = (s32[384,128]{1,0:T(8,128)S(1)}, s32[384,128]{1,0:T(8,128)}, u32[]{:S(2)}) copy-start(s32[384,128]{1,0:T(8,128)} %mask_ref.1) | copy-start | bytes 589828
  13.8 8.1 %copy-start.14 = (bf16[384,768]{1,0:T(8,128)(2,1)S(1)}, bf16[384,768]{1,0:T(8,128)(2,1)}, u32[]{:S(2)}) copy-start(bf16[384,768]{1,0:T(8,128)(2,1)} %constant.15.clone.half_ref) | copy-start | bytes 1769476
  13.8 8.1 %copy-start.17 = (bf16[512,256]{1,0:T(8,128)(2,1)S(1)}, bf16[512,256]{1,0:T(8,128)(2,1)}, u32[]{:S(2)}) copy-start(bf16[512,256]{1,0:T(8,128)(2,1)} %constant.16.clone.z_ref) | copy-start | bytes 786436
  21.9 1.4 %copy-start.5 = (bf16[8,2,1,384,128]{4,3,2,1,0:T(8,128)(2,1)S(1)}, bf16[8,2,1,384,128]{4,3,2,1,0:T(8,128)(2,1)}, u32[]{:S(2)}) copy-start(bf16[8,2,1,384,128]{4,3,2,1,0:T(8,128)(2,1)} %measured_ref.1) | copy-start | bytes 4718596
  28.2 11.7 %all-to-all-start.1 = ((bf16[32,8,384]{2,1,0:T(8,128)(2,1)}), bf16[32,8,384]{2,1,0:T(8,128)(2,1)S(1)}, u32[]{:S(2)}, u32[]{:S(2)}) async-start(bf16[32,8,384]{2,1,0:T(8,128)(2,1)} %shard_map.174.refs_12_), calls=%async_computation.1 | async-start | bytes 393216 | tf_op jit(solution)/shard_map/all_to_all | solution.py:404
  30.7 1.0 %copy-start.16 = (bf16[240,960]{1,0:T(8,128)(2,1)S(1)}, bf16[240,960]{1,0:T(8,128)(2,1)}, u32[]{:S(2)}) copy-start(bf16[240,960]{1,0:T(8,128)(2,1)} %constant.13.clone.refs_3_) | copy-start | bytes 1382404
  31.7 8.2 %copy-start.2 = (f32[4,2,16,384]{3,2,1,0:T(8,128)S(1)}, f32[4,2,16,384]{3,2,1,0:T(8,128)}, u32[]{:S(2)}) copy-start(f32[4,2,16,384]{3,2,1,0:T(8,128)} %noise_ref.1) | copy-start | bytes 589828
  31.7 8.2 %copy-start.3 = (bf16[128,256]{1,0:T(8,128)(2,1)S(1)}, bf16[128,256]{1,0:T(8,128)(2,1)}, u32[]{:S(2)}) copy-start(bf16[128,256]{1,0:T(8,128)(2,1)} %constant.17.clone.order_ref) | copy-start | bytes 196612
where the time goes:
time: 41.2 us; the launch traced here: 40.8 us
  Pallas kernels  16.3 us (40%)
  starting transfers between devices  12.2 us (30%)
  waiting for transfers between devices  6.84 us (17%)
  local copies, waits for them, and re-layouts  5.2 us (13%)
    pallas_call x2, Pallas kernels, score(): call(lambda *refs: score_kernel(z_from, count, len(sources), len(ordered)...  9.4 us
    unnamed x40, local copies, waits for them, and re-layouts  5.2 us
    all_to_all x1, starting transfers between devices, on_device(): lax.all_to_all(blocks, both, split_axis=0, concat_axis=0, tiled=True)  5.12 us
    pallas_call x1, Pallas kernels, on_device(): call(adjoint_kernel, block, [pltpu.VMEM((2 * cols, 2 * cols), BF16)], flo...  4.86 us
    ppermute x1, starting transfers between devices, on_device(): high = lax.ppermute(high, both, across)  4.47 us
    all_to_all x1, waiting for transfers between devices, on_device(): lax.all_to_all(partial, both, split_axis=0, concat_axis=0, tiled=True)  3.46 us
    all_to_all x1, waiting for transfers between devices, on_device(): lax.all_to_all(blocks, both, split_axis=0, concat_axis=0, tiled=True)  3.38 us
    all_to_all x1, starting transfers between devices, on_device(): lax.all_to_all(partial, both, split_axis=0, concat_axis=0, tiled=True)  2.51 us
  transfers between devices with their start and end apart: 4, of which 2 were waited for; matrix products, arithmetic and copies ran while one was open for 0% of the time, Pallas kernels for 23%

commit v1 on v0

v1 whole, which is shorter than its diff:
```python
import functools

import jax
import jax.numpy as jnp
import numpy as np
from jax import lax
from jax.experimental import pallas as pl
from jax.experimental.pallas import tpu as pltpu
from jax.sharding import PartitionSpec as P

STEP_SIZE = 0.5
F32 = jnp.float32
BF16 = jnp.bfloat16
QUAD = 4
GROUP = 8
VMEM_LIMIT = 24 * 2**20
WIDE_LIMIT = 100 * 2**19
BUSY = 4 * 10**10
SHORT = BUSY
BAND = 64


def dot(lhs, rhs):
    return jnp.dot(lhs, rhs, preferred_element_type=F32)


def dot_tn(lhs, rhs):
    return lax.dot_general(lhs, rhs, (((0,), (0,)), ((), ())), preferred_element_type=F32)


def dot_nt(lhs, rhs):
    return lax.dot_general(lhs, rhs, (((1,), (1,)), ((), ())), preferred_element_type=F32)


def dft_table(length):
    index = np.arange(length)
    turns = (index[:, None] * index[None, :]) % length
    angle = turns * (2.0 * np.pi / length)
    scale = 1.0 / np.sqrt(length)
    cos = np.cos(angle) * scale
    sin = np.sin(angle) * scale
    return np.block([[cos, sin], [-sin, cos]]).astype(np.float32).astype(BF16)


def depth_order(devices, x_local, slices):
    depth = devices * slices
    place = np.zeros((x_local, devices * x_local * slices * 2, 2 * depth), np.float32)
    for d in range(devices):
        for x in range(x_local):
            for z in range(slices):
                for p in range(2):
                    place[x, ((d * x_local + x) * slices + z) * 2 + p, p * depth + d * slices + z] = 1
    return place.reshape(-1, 2 * depth).astype(BF16)


def gather_order(slabs, coils, x_local, slices):
    rows = slabs * x_local
    place = np.zeros((slices * 2 * rows, slabs * coils * x_local * slices * 2), np.float32)
    for s in range(slabs):
        for c in range(coils):
            for x in range(x_local):
                for z in range(slices):
                    for p in range(2):
                        source = (((s * coils + c) * x_local + x) * slices + z) * 2 + p
                        place[(z * 2 + p) * rows + s * x_local + x, source] = 1
    return place.astype(BF16)


def first_order():
    place = np.zeros((3, 5, 2, 8, 256), np.float32)
    for a in range(3):
        for b in range(3):
            for o in range(5):
                for p in range(2):
                    place[a, o, p, b, ((o * 3 + b) * 2 + p) * GROUP + 1 + a] = 0.5
    return place.reshape(240, 256).astype(BF16)


def last_order():
    place = np.zeros((QUAD, 3, 2, GROUP, 3, 3, 8), np.float32)
    for xo in range(QUAD):
        for j in range(GROUP):
            a = xo - j + 3
            if 0 <= a < 3:
                for b in range(3):
                    for o in range(2):
                        place[xo, b, o, j, a, b, o] = 1
    return place.reshape(QUAD * 48, 72).astype(BF16)


VMEM = pl.BlockSpec(memory_space=pltpu.VMEM)
HBM = pl.BlockSpec(memory_space=pltpu.HBM)


def call(kernel, out_shape, scratch=(), flops=0, nbytes=0, limit=VMEM_LIMIT, **kwargs):
    return pl.pallas_call(
        kernel,
        out_shape=out_shape,
        scratch_shapes=list(scratch),
        compiler_params=pltpu.CompilerParams(vmem_limit_bytes=limit),
        cost_estimate=pl.CostEstimate(flops=flops, bytes_accessed=nbytes, transcendentals=0),
        **kwargs,
    )


def pack_kernel(image_ref, blocks_ref):
    slices, parts, rows, cols = image_ref.shape
    copies = blocks_ref.shape[0] * blocks_ref.shape[1] // (slices * parts * rows)
    image = image_ref[...].astype(BF16)
    count = slices * parts * rows
    after = lax.broadcasted_iota(jnp.int32, (count, count), 0)
    before = lax.broadcasted_iota(jnp.int32, (count, count), 1)
    source = lax.rem(after, slices * parts) * rows + lax.div(after, slices * parts)
    order = jnp.where(source == before, 1.0, 0.0).astype(BF16)
    moved = dot(order, image.reshape(count, cols))
    slabs = blocks_ref.shape[0] // copies
    moved = moved.reshape(slabs, 1, blocks_ref.shape[1], cols)
    moved = jnp.broadcast_to(moved, (slabs, copies) + moved.shape[2:])
    blocks_ref[...] = moved.reshape(blocks_ref.shape).astype(BF16)


def halo_kernel(outward, image_ref, after_ref, out_ref):
    del after_ref
    slices = image_ref.shape[0]
    even = lax.axis_index("coil") % 2 == 0
    out_ref[...] = jnp.where(even != outward, image_ref[slices - 2 :], image_ref[:2]).astype(BF16)


def fold_weights(sources, targets, rows):
    first_order_ref, last_order_ref, first_ref, b1_ref, second_ref, b2_ref, third_ref, b3_ref, last_ref = sources
    w1_ref, c1_ref, w2_ref, c2_ref, w3_ref, c3_ref, w4_ref = targets
    width = second_ref.shape[0]

    def padded(ref):
        rows[...] = jnp.zeros_like(rows)
        outer, inner, count, _ = ref.shape
        for i in range(outer):
            for j in range(inner):
                rows[i * inner + j, :count] = ref[i, j].astype(F32)
        return rows[: outer * inner].reshape(outer * inner * 8, width).astype(BF16)

    placed = dot_tn(padded(first_ref), first_order_ref[...])
    for xo in range(QUAD):
        moved = pltpu.roll(placed, xo, 1) if xo else placed
        w1_ref[xo * width : (xo + 1) * width] = moved[:, :240].astype(BF16)
    placed = dot(last_order_ref[...], padded(last_ref)).astype(BF16)
    for xo in range(QUAD):
        w4_ref[:, xo * width : (xo + 1) * width] = placed[xo * 48 : (xo + 1) * 48]
    for source, target in ((second_ref, w2_ref), (third_ref, w3_ref)):
        turned = (jnp.transpose(source[...].astype(F32)) * 0.5).astype(BF16)
        zeros = jnp.zeros_like(turned)
        target[...] = jnp.concatenate(
            [jnp.concatenate([turned, zeros], axis=1), jnp.concatenate([zeros, turned], axis=1)], axis=0
        )
    for source, target in ((b1_ref, c1_ref), (b2_ref, c2_ref), (b3_ref, c3_ref)):
        target[...] = jnp.transpose(jnp.broadcast_to(source[...] * 0.5, (width, width)))


def staggered(chains):
    waiting, running = list(chains), []
    while waiting or running:
        if waiting:
            running.append(waiting.pop(0))
        for one in running[::-1]:
            if next(one, one) is one:
                running.remove(one)


def half_silu(half):
    return (half + half * jnp.tanh(half)).astype(BF16)


def score_kernel(starts, z_count, sources, n_ordered, *refs):
    refs, out_ref, scratch = refs[:sources], refs[sources + n_ordered], refs[sources + n_ordered + 1 :]
    folded, rows, scratch = scratch[:7], scratch[7], scratch[8:]
    fold_weights(refs[3:], folded, rows)
    score_slices(starts, z_count, refs[:3], folded, out_ref, *scratch)


def score_slices(starts, z_count, planes, weights, out_ref, shifted, windows):
    image_ref, low_ref, high_ref = planes
    w1_ref, c1_ref, w2_ref, c2_ref, w3_ref, c3_ref, w4_ref = weights
    slices, _, rows, cols = image_ref.shape
    quads = rows // QUAD
    width = c1_ref.shape[0]
    even = lax.axis_index("coil") % 2 == 0

    def plane_at(z, p, below_ref, above_ref):
        if 0 <= z < slices:
            return image_ref[z, p].astype(BF16).astype(F32)
        ref, at = (below_ref, z + 2) if z < 0 else (above_ref, z - slices)
        return ref[at, p].astype(F32)

    def plane(i, p):
        return jnp.where(
            even,
            plane_at(starts[0] + i - 2, p, high_ref, low_ref),
            plane_at(starts[1] + i - 2, p, low_ref, high_ref),
        )

    def earlier(values):
        at = lax.broadcasted_iota(jnp.int32, values.shape, 1)
        return jnp.where(at == 0, 0.0, pltpu.roll(values, 1, 1))

    def later(values):
        at = lax.broadcasted_iota(jnp.int32, values.shape, 1)
        return jnp.where(at == cols - 1, 0.0, pltpu.roll(values, cols - 1, 1))

    shifted[...] = jnp.zeros_like(shifted)
    for i in range(z_count + 4):
        for p in range(2):
            values = plane(i, p)
            for b, moved in enumerate((earlier(values), values, later(values))):
                shifted[b, 4 : 4 + rows] = moved
                for q in range(quads):
                    start = QUAD * q + 2
                    windows[q, i, b, p * GROUP : (p + 1) * GROUP] = shifted[b, start : start + GROUP].astype(BF16)

    spots = [(q, z) for z in range(z_count) for q in range(quads)]
    inputs = jnp.concatenate([windows[q, z : z + 5].reshape(240, cols) for q, z in spots], axis=1)
    taps = {}
    fields = {}
    row = lax.broadcasted_iota(jnp.int32, (GROUP, cols), 0)

    def add_spot(i):
        q, z = spots[i]
        first, last = i * cols, (i + 1) * cols
        part = jnp.concatenate(
            [
                taps[n][:, max(first, n) - n : min(last, n + tile) - n]
                for n in range(first - first % tile, last, tile)
            ],
            axis=1,
        )
        total = part[16:32] + earlier(part[:16]) + later(part[32:])
        start = QUAD * q - 2
        for o in range(2):
            moved = pltpu.roll(total[o * GROUP : (o + 1) * GROUP], start % GROUP, 0)
            for t, keep in ((start // GROUP, row >= start % GROUP), (start // GROUP + 1, row < start % GROUP)):
                if 0 <= t < rows // GROUP:
                    field = fields.get((z, o, t))
                    piece = jnp.where(keep, moved, 0.0)
                    fields[z, o, t] = piece if field is None else field + piece
        if q == quads - 1:
            for o in range(2):
                for t in range(rows // GROUP):
                    out_ref[z, o, t * GROUP : (t + 1) * GROUP] = fields.pop((z, o, t))

    def bias(ref, lanes):
        return jnp.concatenate([jnp.concatenate([ref[...]] * (lanes // 128), axis=1)] * 2, axis=0)

    def chain(start, stop, pair):
        half = slice(2 * width * pair, 2 * width * (pair + 1))
        lanes = stop - start
        total = dot(w1_ref[half], inputs[:, start:stop])
        yield
        hidden = half_silu(total + bias(c1_ref, lanes))
        yield
        total = dot(w2_ref[...], hidden)
        yield
        hidden = half_silu(total + bias(c2_ref, lanes))
        yield
        total = dot(w3_ref[...], hidden)
        yield
        hidden = half_silu(total + bias(c3_ref, lanes))
        yield
        part = dot(w4_ref[:, half], hidden)
        if pair == 0:
            taps[start] = part
            return
        taps[start] = taps[start] + part
        while done[0] < len(spots) and stop >= (done[0] + 1) * cols:
            add_spot(done[0])
            done[0] += 1

    done = [0]
    length = len(spots) * cols
    tile = 256
    staggered([chain(n, min(n + tile, length), pair) for n in range(0, length, tile) for pair in range(QUAD // 2)])

def adjoint_kernel(
    planes_ref, sens_ref, measured_hbm, mask_ref, half_ref, z_ref, out_ref, y_ref, measured_ref, sems
):
    blocks, block_rows, cols = planes_ref.shape
    coils, _, x_local, _, depth = sens_ref.shape
    per = max(1, 512 // depth)
    groups = [range(c, min(c + per, coils)) for c in range(0, coils, per)]
    arrivals = {}
    for i, group in enumerate(groups):
        part = pl.ds(group[0], len(group))
        arrivals[group] = pltpu.make_async_copy(measured_hbm.at[part], measured_ref.at[part], sems.at[i])
        arrivals[group].start()
    y_ref[:cols] = half_ref[...]
    y_ref[cols:, :cols] = -half_ref[:, cols:]
    y_ref[cols:, cols:] = half_ref[:, :cols]
    received = planes_ref[...].astype(F32).reshape(blocks * block_rows, cols).astype(BF16)
    z_table = z_ref[: 2 * depth]
    result = None
    for x in range(x_local):
        place = z_ref[2 * depth + x * blocks * block_rows : 2 * depth + (x + 1) * blocks * block_rows]
        planes = dot_tn(received, place)
        image_real = planes[:, :depth]
        image_imag = planes[:, depth:]
        totals = {}

        def along_z(half, count):
            for i in range(count):
                at = slice(i * depth, (i + 1) * depth)
                yield dot(jnp.concatenate([half[:cols, at], half[cols:, at]], axis=1), z_table)

        def stack(top, bottom):
            return jnp.concatenate([jnp.concatenate(top, axis=1), jnp.concatenate(bottom, axis=1)], axis=0)

        bands = [slice(r, min(r + BAND, cols)) for r in range(0, cols, BAND)]

        def chain(group):
            reals = {c: [] for c in group}
            imags = {c: [] for c in group}

            def joined(parts):
                return [jnp.concatenate(parts[c], axis=0) for c in group]

            for band in bands:
                for c in group:
                    sens_real = sens_ref[c, 0, x, band].astype(F32)
                    sens_imag = sens_ref[c, 1, x, band].astype(F32)
                    reals[c].append((sens_real * image_real[band] - sens_imag * image_imag[band]).astype(BF16))
                    imags[c].append((sens_real * image_imag[band] + sens_imag * image_real[band]).astype(BF16))
            stacked = stack(joined(reals), joined(imags))
            yield
            half = dot(y_ref[...], stacked).astype(BF16)
            yield
            specs = list(along_z(half, len(group)))
            yield
            if x == 0:
                arrivals[group].wait()
            reals = {c: [] for c in group}
            imags = {c: [] for c in group}
            for band in bands:
                sampled = mask_ref[band].astype(F32)
                for spec, c in zip(specs, group):
                    measured_real = measured_ref[c, 0, x, band].astype(F32)
                    measured_imag = measured_ref[c, 1, x, band].astype(F32)
                    reals[c].append((sampled * (spec[band, :depth] - measured_real)).astype(BF16))
                    imags[c].append((sampled * (spec[band, depth:] - measured_imag)).astype(BF16))
            stacked = stack(joined(imags), joined(reals))
            yield
            half = dot(y_ref[...], stacked).astype(BF16)
            yield
            backs = list(along_z(half, len(group)))
            yield
            for band in bands:
                real = imag = None
                for back, c in zip(backs, group):
                    back_imag = back[band, :depth]
                    back_real = back[band, depth:]
                    sens_real = sens_ref[c, 0, x, band].astype(F32)
                    sens_imag = sens_ref[c, 1, x, band].astype(F32)
                    one = sens_real * back_real + sens_imag * back_imag
                    two = sens_real * back_imag - sens_imag * back_real
                    real, imag = (one, two) if real is None else (real + one, imag + two)
                totals.setdefault(band.start, []).append((real, imag))

        staggered([chain(group) for group in groups])
        total = jnp.concatenate(
            [
                jnp.concatenate([sum(t[part] for t in totals[band.start]) for part in range(2)], axis=1)
                for band in bands
            ],
            axis=0,
        ).astype(BF16)
        placed = dot_nt(place, total)
        result = placed if result is None else result + placed
    out_ref[...] = result.reshape(out_ref.shape).astype(BF16)


def final_kernel(image_ref, noise_ref, one_ref, two_ref, back_ref, order_ref, out_ref):
    blocks, block_rows, cols = back_ref.shape
    received = back_ref[...].astype(F32).reshape(blocks * block_rows, cols).astype(BF16)
    gradient = dot(order_ref[...], received).reshape(image_ref.shape)
    slices = image_ref.shape[0]
    cut = one_ref.shape[0]
    even = lax.axis_index("coil") % 2 == 0
    for z in range(slices):
        at_even = two_ref[z] if z < slices - cut else one_ref[z - (slices - cut)]
        at_odd = one_ref[z] if z < cut else two_ref[z - cut]
        field = jnp.where(even, at_even, at_odd)
        out_ref[z] = image_ref[z] + STEP_SIZE * (field - gradient[z]) + noise_ref[z]


def on_device(
    image, noise, sens, measured, mask, w_first, b_first, w_second, b_second, w_third, b_third, w_last
):
    slabs = lax.axis_size("slab")
    groups = lax.axis_size("coil")
    devices = slabs * groups
    slices, _, rows, cols = image.shape
    x_local = rows // slabs
    width = w_second.shape[0]
    depth = sens.shape[4]
    both = ("slab", "coil")
    block = jax.ShapeDtypeStruct((devices, x_local * slices * 2, cols), BF16)

    blocks = call(pack_kernel, block, flops=BUSY, nbytes=10**6, in_specs=[VMEM])(image)
    pairs = [(i, i ^ 1) for i in range(devices)]
    across = [(i, ((i + 1) ^ 1) - 1) for i in range(1, devices - 1)]

    def halo(outward, after):
        kernel = functools.partial(halo_kernel, outward)
        shape = jax.ShapeDtypeStruct((2, 2, rows, cols), BF16)
        slab = call(
            kernel, shape, flops=BUSY, nbytes=10**6, in_specs=[VMEM, pl.BlockSpec(memory_space=pl.ANY)]
        )(image, after)
        return lax.ppermute(slab, both, across if outward else pairs)

    low = halo(False, blocks)
    planes = lax.all_to_all(blocks, both, split_axis=0, concat_axis=0, tiled=True)

    cut = max(1, slices // 4)
    weights = (
        jnp.asarray(first_order()), jnp.asarray(last_order()),
        jnp.transpose(w_first, (0, 2, 1, 3)), b_first[None],
        w_second, b_second[None], w_third, b_third[None], w_last,
    )

    def score(starts, count, flops, planes, *ordered):
        sources = planes + weights
        return call(
            lambda *refs: score_kernel(starts, count, len(sources), len(ordered), *refs),
            jax.ShapeDtypeStruct((count, 2, rows, cols), F32),
            [
                pltpu.VMEM((QUAD * width, 240), BF16),
                pltpu.VMEM((width, width), F32),
                pltpu.VMEM((2 * width, 2 * width), BF16),
                pltpu.VMEM((width, width), F32),
                pltpu.VMEM((2 * width, 2 * width), BF16),
                pltpu.VMEM((width, width), F32),
                pltpu.VMEM((48, QUAD * width), BF16),
                pltpu.VMEM((30, 8, width), F32),
                pltpu.VMEM((3, rows + 8, cols), F32),
                pltpu.VMEM((rows // QUAD, count + 4, 3, 2 * GROUP, cols), BF16),
            ],
            flops=flops,
            nbytes=2 * 10**6,
            in_specs=[VMEM] * len(sources) + [pl.BlockSpec(memory_space=pl.ANY)] * len(ordered),
        )(*sources, *ordered)

    apart = slices - cut >= 2
    high = None if apart else halo(True, blocks)
    score_one = score((slices - cut, 0), cut, SHORT, (image, low, low if apart else high))
    if apart:
        high = halo(True, score_one)
    z_tables = np.concatenate([dft_table(depth).T, depth_order(devices, x_local, slices)], axis=0)
    partial = call(
        adjoint_kernel, block, [pltpu.VMEM((2 * cols, 2 * cols), BF16), pltpu.VMEM(measured.shape, BF16),
         pltpu.SemaphoreType.DMA((sens.shape[0],))],
        flops=BUSY, nbytes=5 * 10**6, limit=WIDE_LIMIT, in_specs=[VMEM] * 2 + [HBM] + [VMEM] * 3
    )(planes, sens, measured, mask, jnp.asarray(dft_table(cols)[:cols]), jnp.asarray(z_tables))
    score_two = score((0, cut), slices - cut, BUSY, (image, low, high), partial)
    back = lax.all_to_all(partial, both, split_axis=0, concat_axis=0, tiled=True)
    return call(final_kernel, jax.ShapeDtypeStruct(image.shape, F32), nbytes=10**6)(
        image, noise, score_one, score_two, back,
        jnp.asarray(gather_order(slabs, groups, x_local, slices)),
    )


def solution(mesh):
    whole = P(("slab", "coil"), None, None, None)
    by_coil = P("coil", None, "slab", None, None)
    return jax.shard_map(
        on_device,
        mesh=mesh,
        in_specs=(whole, whole, by_coil, by_coil) + (P(),) * 8,
        out_specs=whole,
        check_vma=False,
    )
```

time: 41.2 us -> 36.6 us (0.89)
  local copies, waits for them, and re-layouts: 5.2 us -> 1.97 us
  waiting for transfers between devices: 6.84 us -> 4.29 us
  starting transfers between devices: 12.2 us -> 13.5 us
    unnamed x40 -> x36, local copies, waits for them, and re-layouts: 5.2 us -> 1.97 us
    all_to_all x1, starting transfers between devices: 5.12 us -> 7.15 us  [on_device(): lax.all_to_all(blocks, both, split_axis=0, concat_axis=0, tiled=True)]
    all_to_all x1, waiting for transfers between devices: 3.46 us -> 1.52 us  [on_device(): lax.all_to_all(partial, both, split_axis=0, concat_axis=0, tiled=True)]
    ppermute x2, starting transfers between devices: 4.59 us -> 3.8 us  [halo(): return lax.ppermute(slab, both, across if outward else pairs)]
    all_to_all x1, waiting for transfers between devices: 3.38 us -> 2.76 us  [on_device(): lax.all_to_all(blocks, both, split_axis=0, concat_axis=0, tiled=True)]
    pallas_call x4 -> x6, Pallas kernels: 15.4 us -> 15.4 us  [the longest x2 9.16 us: score(): call(lambda *refs: score_kernel(starts, count, len(sources), len(ordered)...]
  transfers between devices with their start and end apart: 4 -> 4, of which waited for: 2 -> 2; matrix products, arithmetic and copies ran while one was open for 0% -> 0% of each run, Pallas kernels for 23% -> 40%
where the time goes in v1:
time: 36.6 us; the launch traced here: 36.3 us
  Pallas kernels  16.3 us (45%)
  starting transfers between devices  13.5 us (37%)
  waiting for transfers between devices  4.29 us (12%)
  local copies, waits for them, and re-layouts  1.97 us (5%)
    pallas_call x2, Pallas kernels, score(): call(lambda *refs: score_kernel(starts, count, len(sources), len(ordered)...  9.16 us
    all_to_all x1, starting transfers between devices, on_device(): lax.all_to_all(blocks, both, split_axis=0, concat_axis=0, tiled=True)  7.15 us
    pallas_call x1, Pallas kernels, on_device(): call(adjoint_kernel, block, [pltpu.VMEM((2 * cols, 2 * cols), BF16), pltp...  5.39 us
    ppermute x2, starting transfers between devices, halo(): return lax.ppermute(slab, both, across if outward else pairs)  3.8 us
    all_to_all x1, waiting for transfers between devices, on_device(): lax.all_to_all(blocks, both, split_axis=0, concat_axis=0, tiled=True)  2.76 us
    all_to_all x1, starting transfers between devices, on_device(): lax.all_to_all(partial, both, split_axis=0, concat_axis=0, tiled=True)  2.52 us
    unnamed x36, local copies, waits for them, and re-layouts  1.97 us
    all_to_all x1, waiting for transfers between devices, on_device(): lax.all_to_all(partial, both, split_axis=0, concat_axis=0, tiled=True)  1.52 us
  transfers between devices with their start and end apart: 4, of which 2 were waited for; matrix products, arithmetic and copies ran while one was open for 0% of the time, Pallas kernels for 40%

profile of v1, /device:TPU:1, one launch (start us, length us, event | category | flops | bytes accessed | tf_op | source)
XLA Modules:
  0.0 36.3 jit_solution(10225839398810767180)
XLA Ops:
  0.0 0.9 %copy-done = f32[4,2,16,384]{3,2,1,0:T(8,128)S(1)} copy-done((f32[4,2,16,384]{3,2,1,0:T(8,128)S(1)}, f32[4,2,16,384]{3,2,1,0:T(8,128)}, u32[]{:S(2)}) %copy-start) | copy-done | bytes 196632
  0.9 0.9 %shard_map.163.after_ref = bf16[32,8,384]{2,1,0:T(8,128)(2,1)} custom-call(f32[4,2,16,384]{3,2,1,0:T(8,128)S(1)} %copy-done), custom_call_target="tpu_custom_call" | custom-call | flops 40000000000 | bytes 1000000 | tf_op jit(solution)/shard_map/pallas_call | solution.py:404
  1.8 0.0 copy-start.9
  1.8 0.0 copy-start.11
  1.8 0.0 copy-start.12
  1.8 0.0 copy-start.15
  1.9 0.0 copy-start.17
  1.9 0.1 collective-permute-start
  2.0 7.2 %all-to-all-start = ((bf16[32,8,384]{2,1,0:T(8,128)(2,1)}), bf16[32,8,384]{2,1,0:T(8,128)(2,1)S(1)}, u32[]{:S(2)}, u32[]{:S(2)}) async-start(bf16[32,8,384]{2,1,0:T(8,128)(2,1)} %shard_map.163.after_ref), calls=%async_computation | async-start | bytes 393216 | tf_op jit(solution)/shard_map/all_to_all | solution.py:417
  9.3 2.7 %shard_map.165.after_ref.one_ref = f32[1,2,16,384]{3,2,1,0:T(8,128)S(1)} custom-call(f32[4,2,16,384]{3,2,1,0:T(8,128)S(1)} %copy-done.1, bf16[2,2,16,384]{3,2,1,0:T(8,128)(2,1)S(1)} %collective-permute-done.refs_1_.refs_2_, bf16[2,2,16,384]{3,2,1,0:T(8,128)(2,1)S(1)} %collective-permute-done.refs_1_.refs_2_, bf16[240,256]{1,0:T(8,128)(2,1)S(1)} %copy-done.15, ...), custom_call_target="tpu_custom_call" | custom-call | flops 40000000000 | bytes 2000000 | tf_op jit(solution)/shard_map/pallas_call | solution.py:428
  12.0 0.0 copy-start.4
  12.0 0.0 copy-start.5
  12.0 0.0 copy-start.13
  12.0 0.0 copy-start.14
  12.1 3.7 %collective-permute-start.1 = (bf16[2,2,16,384]{3,2,1,0:T(8,128)(2,1)S(1)}, bf16[2,2,16,384]{3,2,1,0:T(8,128)(2,1)S(1)}, u32[]{:S(2)}, u32[]{:S(2)}) collective-permute-start(bf16[2,2,16,384]{3,2,1,0:T(8,128)(2,1)S(1)} %shard_map.166), channel_id=1, source_target_pairs={{1,2},{2,1},{3,4},{4,3},{5,6},{6,5},{7,8},{8,7},{9,10},{10,9},{11,... | collective-permute-start | bytes 147464 | tf_op jit(solution)/shard_map/ppermute | solution.py:414
  15.7 2.8 %all-to-all-done.planes_ref = bf16[32,8,384]{2,1,0:T(8,128)(2,1)S(1)} async-done(((bf16[32,8,384]{2,1,0:T(8,128)(2,1)}), bf16[32,8,384]{2,1,0:T(8,128)(2,1)S(1)}, u32[]{:S(2)}, u32[]{:S(2)}) %all-to-all-start) | async-done | bytes 196640 | tf_op jit(solution)/shard_map/all_to_all | solution.py:417
  18.5 5.4 %shard_map.167.refs_12_ = bf16[32,8,384]{2,1,0:T(8,128)(2,1)} custom-call(bf16[32,8,384]{2,1,0:T(8,128)(2,1)S(1)} %all-to-all-done.planes_ref, bf16[8,2,1,384,128]{4,3,2,1,0:T(8,128)(2,1)S(1)} %copy-done.4, bf16[8,2,1,384,128]{4,3,2,1,0:T(8,128)(2,1)} %measured_hbm.1, s32[384,128]{1,0:T(8,128)S(1)} %copy-done.5, bf16[384,768]{1,0:T(8,128)(2,1)S(1)} %copy-done.13, ...), custom_call_target="tpu_custom_call" | custom-call | flops 40000000000 | bytes 5000000 | tf_op jit(solution)/shard_map/pallas_call | solution.py:454
  23.9 2.5 %all-to-all-start.1 = ((bf16[32,8,384]{2,1,0:T(8,128)(2,1)}), bf16[32,8,384]{2,1,0:T(8,128)(2,1)S(1)}, u32[]{:S(2)}, u32[]{:S(2)}) async-start(bf16[32,8,384]{2,1,0:T(8,128)(2,1)} %shard_map.167.refs_12_), calls=%async_computation.1 | async-start | bytes 393216 | tf_op jit(solution)/shard_map/all_to_all | solution.py:460
  26.5 0.0 copy-start.3
  26.5 0.0 copy-start.16
  26.5 0.9 %copy-done.16 = bf16[240,256]{1,0:T(8,128)(2,1)S(1)} copy-done((bf16[240,256]{1,0:T(8,128)(2,1)S(1)}, bf16[240,256]{1,0:T(8,128)(2,1)}, u32[]{:S(2)}) %copy-start.16) | copy-done | bytes 122904
  27.4 6.5 %shard_map.168.two_ref = f32[3,2,16,384]{3,2,1,0:T(8,128)S(1)} custom-call(f32[4,2,16,384]{3,2,1,0:T(8,128)S(1)} %copy-done.1, bf16[2,2,16,384]{3,2,1,0:T(8,128)(2,1)S(1)} %collective-permute-done.refs_1_.refs_2_, bf16[2,2,16,384]{3,2,1,0:T(8,128)(2,1)S(1)} %collective-permute-done.1.refs_2_, bf16[240,256]{1,0:T(8,128)(2,1)S(1)} %copy-done.16, ...), custom_call_target="tpu_custom_call" | custom-call | flops 40000000000 | bytes 2000000 | tf_op jit(solution)/shard_map/pallas_call | solution.py:428
  33.9 1.5 %all-to-all-done.1.back_ref = bf16[32,8,384]{2,1,0:T(8,128)(2,1)S(1)} async-done(((bf16[32,8,384]{2,1,0:T(8,128)(2,1)}), bf16[32,8,384]{2,1,0:T(8,128)(2,1)S(1)}, u32[]{:S(2)}, u32[]{:S(2)}) %all-to-all-start.1) | async-done | bytes 196640 | tf_op jit(solution)/shard_map/all_to_all | solution.py:460
  35.4 0.9 %shard_map.169 = f32[4,2,16,384]{3,2,1,0:T(8,128)} custom-call(f32[4,2,16,384]{3,2,1,0:T(8,128)S(1)} %copy-done.1, f32[4,2,16,384]{3,2,1,0:T(8,128)S(1)} %copy-done.2, f32[1,2,16,384]{3,2,1,0:T(8,128)S(1)} %shard_map.165.after_ref.one_ref, f32[3,2,16,384]{3,2,1,0:T(8,128)S(1)} %shard_map.168.two_ref, bf16[32,8,384]{2,1,0:T(8,128)(2,1)S(1)} %all-to-all-done.1.back_ref, ...), custom_call_target="tpu_custom_call" | custom-call | bytes 1000000 | tf_op jit(solution)/shard_map/pallas_call | solution.py:461
  (27 shorter events, 0.1 us)
Async XLA Ops:
  0.0 0.9 %copy-start = (f32[4,2,16,384]{3,2,1,0:T(8,128)S(1)}, f32[4,2,16,384]{3,2,1,0:T(8,128)}, u32[]{:S(2)}) copy-start(f32[4,2,16,384]{3,2,1,0:T(8,128)} %image_ref.7) | copy-start | bytes 589828
  1.8 7.4 %copy-start.1 = (f32[4,2,16,384]{3,2,1,0:T(8,128)S(1)}, f32[4,2,16,384]{3,2,1,0:T(8,128)}, u32[]{:S(2)}) copy-start(f32[4,2,16,384]{3,2,1,0:T(8,128)} %image_ref.7) | copy-start | bytes 589828
  1.8 7.4 %copy-start.6 = (bf16[128,128]{1,0:T(8,128)(2,1)S(1)}, bf16[128,128]{1,0:T(8,128)(2,1)}, u32[]{:S(2)}) copy-start(bf16[128,128]{1,0:T(8,128)(2,1)} %refs_7_.3) | copy-start | bytes 98308
  1.8 7.4 %copy-start.7 = (bf16[128,128]{1,0:T(8,128)(2,1)S(1)}, bf16[128,128]{1,0:T(8,128)(2,1)}, u32[]{:S(2)}) copy-start(bf16[128,128]{1,0:T(8,128)(2,1)} %refs_9_.3) | copy-start | bytes 98308
  1.8 7.4 %copy-start.8 = (bf16[3,3,10,128]{3,1,2,0:T(4,128)(2,1)S(1)}, bf16[3,3,10,128]{3,1,2,0:T(4,128)(2,1)}, u32[]{:S(2)}) copy-start(bf16[3,3,10,128]{3,1,2,0:T(4,128)(2,1)} %param.22) | copy-start | bytes 69124
  1.8 7.4 %copy-start.9 = (bf16[3,3,2,128]{3,2,1,0:T(2,128)(2,1)S(1)}, bf16[3,3,2,128]{3,2,1,0:T(2,128)(2,1)}, u32[]{:S(2)}) copy-start(bf16[3,3,2,128]{3,2,1,0:T(2,128)(2,1)} %refs_11_.3) | copy-start | bytes 13828
  1.8 7.4 %copy-start.10 = (f32[128]{0:T(128)S(1)}, f32[128]{0:T(128)}, u32[]{:S(2)}) copy-start(f32[128]{0:T(128)} %param.23) | copy-start | bytes 1540
  1.8 7.4 %copy-start.11 = (f32[128]{0:T(128)S(1)}, f32[128]{0:T(128)}, u32[]{:S(2)}) copy-start(f32[128]{0:T(128)} %param.25) | copy-start | bytes 1540
  1.8 7.4 %copy-start.12 = (f32[128]{0:T(128)S(1)}, f32[128]{0:T(128)}, u32[]{:S(2)}) copy-start(f32[128]{0:T(128)} %param.27) | copy-start | bytes 1540
  1.8 7.4 %copy-start.15 = (bf16[240,256]{1,0:T(8,128)(2,1)S(1)}, bf16[240,256]{1,0:T(8,128)(2,1)}, u32[]{:S(2)}) copy-start(bf16[240,256]{1,0:T(8,128)(2,1)} %constant.10.clone.refs_3_) | copy-start | bytes 368644
  1.9 7.4 %copy-start.17 = (bf16[192,72]{1,0:T(8,128)(2,1)S(1)}, bf16[192,72]{1,0:T(8,128)(2,1)}, u32[]{:S(2)}) copy-start(bf16[192,72]{1,0:T(8,128)(2,1)} %constant.11.clone.refs_4_) | copy-start | bytes 82948
  1.9 7.3 %collective-permute-start = (bf16[2,2,16,384]{3,2,1,0:T(8,128)(2,1)S(1)}, bf16[2,2,16,384]{3,2,1,0:T(8,128)(2,1)S(1)}, u32[]{:S(2)}, u32[]{:S(2)}) collective-permute-start(bf16[2,2,16,384]{3,2,1,0:T(8,128)(2,1)S(1)} %shard_map.164), channel_id=1, source_target_pairs={{0,1},{1,0},{2,3},{3,2},{4,5},{5,4},{6,7},{7,6},{8,9},{9,8},{10,11... | collective-permute-start | bytes 147464 | tf_op jit(solution)/shard_map/ppermute | solution.py:414
  2.0 16.5 %all-to-all-start = ((bf16[32,8,384]{2,1,0:T(8,128)(2,1)}), bf16[32,8,384]{2,1,0:T(8,128)(2,1)S(1)}, u32[]{:S(2)}, u32[]{:S(2)}) async-start(bf16[32,8,384]{2,1,0:T(8,128)(2,1)} %shard_map.163.after_ref), calls=%async_computation | async-start | bytes 393216 | tf_op jit(solution)/shard_map/all_to_all | solution.py:417
  12.0 6.5 %copy-start.4 = (bf16[8,2,1,384,128]{4,3,2,1,0:T(8,128)(2,1)S(1)}, bf16[8,2,1,384,128]{4,3,2,1,0:T(8,128)(2,1)}, u32[]{:S(2)}) copy-start(bf16[8,2,1,384,128]{4,3,2,1,0:T(8,128)(2,1)} %sens_ref.1) | copy-start | bytes 4718596
  12.0 6.5 %copy-start.5 = (s32[384,128]{1,0:T(8,128)S(1)}, s32[384,128]{1,0:T(8,128)}, u32[]{:S(2)}) copy-start(s32[384,128]{1,0:T(8,128)} %mask_ref.1) | copy-start | bytes 589828
  12.0 6.5 %copy-start.13 = (bf16[384,768]{1,0:T(8,128)(2,1)S(1)}, bf16[384,768]{1,0:T(8,128)(2,1)}, u32[]{:S(2)}) copy-start(bf16[384,768]{1,0:T(8,128)(2,1)} %constant.12.clone.half_ref) | copy-start | bytes 1769476
  12.0 6.5 %copy-start.14 = (bf16[512,256]{1,0:T(8,128)(2,1)S(1)}, bf16[512,256]{1,0:T(8,128)(2,1)}, u32[]{:S(2)}) copy-start(bf16[512,256]{1,0:T(8,128)(2,1)} %constant.13.clone.z_ref) | copy-start | bytes 786436
  12.1 14.4 %collective-permute-start.1 = (bf16[2,2,16,384]{3,2,1,0:T(8,128)(2,1)S(1)}, bf16[2,2,16,384]{3,2,1,0:T(8,128)(2,1)S(1)}, u32[]{:S(2)}, u32[]{:S(2)}) collective-permute-start(bf16[2,2,16,384]{3,2,1,0:T(8,128)(2,1)S(1)} %shard_map.166), channel_id=1, source_target_pairs={{1,2},{2,1},{3,4},{4,3},{5,6},{6,5},{7,8},{8,7},{9,10},{10,9},{11,... | collective-permute-start | bytes 147464 | tf_op jit(solution)/shard_map/ppermute | solution.py:414
  23.9 11.5 %all-to-all-start.1 = ((bf16[32,8,384]{2,1,0:T(8,128)(2,1)}), bf16[32,8,384]{2,1,0:T(8,128)(2,1)S(1)}, u32[]{:S(2)}, u32[]{:S(2)}) async-start(bf16[32,8,384]{2,1,0:T(8,128)(2,1)} %shard_map.167.refs_12_), calls=%async_computation.1 | async-start | bytes 393216 | tf_op jit(solution)/shard_map/all_to_all | solution.py:460
  26.5 9.0 %copy-start.2 = (f32[4,2,16,384]{3,2,1,0:T(8,128)S(1)}, f32[4,2,16,384]{3,2,1,0:T(8,128)}, u32[]{:S(2)}) copy-start(f32[4,2,16,384]{3,2,1,0:T(8,128)} %noise_ref.1) | copy-start | bytes 589828
  26.5 9.0 %copy-start.3 = (bf16[128,256]{1,0:T(8,128)(2,1)S(1)}, bf16[128,256]{1,0:T(8,128)(2,1)}, u32[]{:S(2)}) copy-start(bf16[128,256]{1,0:T(8,128)(2,1)} %constant.14.clone.order_ref) | copy-start | bytes 196612
  26.5 1.0 %copy-start.16 = (bf16[240,256]{1,0:T(8,128)(2,1)S(1)}, bf16[240,256]{1,0:T(8,128)(2,1)}, u32[]{:S(2)}) copy-start(bf16[240,256]{1,0:T(8,128)(2,1)} %constant.10.clone.refs_3_) | copy-start | bytes 368644

commit v2 on v1

--- a/solution.py
+++ b/solution.py
@@ -18,6 +18,7 @@
 BUSY = 4 * 10**10
 SHORT = BUSY
 BAND = 64
+EARLY = 2
 
 
 def dot(lhs, rhs):
@@ -66,28 +67,6 @@
     return place.astype(BF16)
 
 
-def first_order():
-    place = np.zeros((3, 5, 2, 8, 256), np.float32)
-    for a in range(3):
-        for b in range(3):
-            for o in range(5):
-                for p in range(2):
-                    place[a, o, p, b, ((o * 3 + b) * 2 + p) * GROUP + 1 + a] = 0.5
-    return place.reshape(240, 256).astype(BF16)
-
-
-def last_order():
-    place = np.zeros((QUAD, 3, 2, GROUP, 3, 3, 8), np.float32)
-    for xo in range(QUAD):
-        for j in range(GROUP):
-            a = xo - j + 3
-            if 0 <= a < 3:
-                for b in range(3):
-                    for o in range(2):
-                        place[xo, b, o, j, a, b, o] = 1
-    return place.reshape(QUAD * 48, 72).astype(BF16)
-
-
 VMEM = pl.BlockSpec(memory_space=pltpu.VMEM)
 HBM = pl.BlockSpec(memory_space=pltpu.HBM)
 
@@ -103,6 +82,12 @@
     )
 
 
+def split(values, count):
+    if count & (count - 1) == 0:
+        return values & (count - 1), lax.shift_right_logical(values, count.bit_length() - 1)
+    return lax.rem(values, count), lax.div(values, count)
+
+
 def pack_kernel(image_ref, blocks_ref):
     slices, parts, rows, cols = image_ref.shape
     copies = blocks_ref.shape[0] * blocks_ref.shape[1] // (slices * parts * rows)
@@ -110,8 +95,9 @@
     count = slices * parts * rows
     after = lax.broadcasted_iota(jnp.int32, (count, count), 0)
     before = lax.broadcasted_iota(jnp.int32, (count, count), 1)
-    source = lax.rem(after, slices * parts) * rows + lax.div(after, slices * parts)
-    order = jnp.where(source == before, 1.0, 0.0).astype(BF16)
+    part, x = split(after, slices * parts)
+    source_x, source_part = split(before, rows)
+    order = jnp.where((part == source_part) & (x == source_x), 1.0, 0.0).astype(BF16)
     moved = dot(order, image.reshape(count, cols))
     slabs = blocks_ref.shape[0] // copies
     moved = moved.reshape(slabs, 1, blocks_ref.shape[1], cols)
@@ -126,9 +112,38 @@
     out_ref[...] = jnp.where(even != outward, image_ref[slices - 2 :], image_ref[:2]).astype(BF16)
 
 
+def by_three(values):
+    return lax.shift_right_logical(values * 11, 5)
+
+
+def first_order():
+    row = lax.broadcasted_iota(jnp.int32, (240, 256), 0)
+    col = lax.broadcasted_iota(jnp.int32, (240, 256), 1)
+    tap = lax.shift_right_logical(row, 3)
+    a = jnp.where(tap >= 20, 2, jnp.where(tap >= 10, 1, 0))
+    channel = tap - 10 * a
+    group = lax.shift_right_logical(col, 3)
+    offset = by_three(lax.shift_right_logical(group, 1))
+    b = lax.shift_right_logical(group, 1) - 3 * offset
+    same = (channel == 2 * offset + (group & 1)) & ((row & 7) == b) & ((col & 7) == a + 1)
+    return jnp.where(same, 0.5, 0.0).astype(BF16)
+
+
+def last_order():
+    row = lax.broadcasted_iota(jnp.int32, (QUAD * 48, 72), 0)
+    col = lax.broadcasted_iota(jnp.int32, (QUAD * 48, 72), 1)
+    group = lax.shift_right_logical(row, 3)
+    xo = by_three(lax.shift_right_logical(group, 1))
+    b = lax.shift_right_logical(group, 1) - 3 * xo
+    tap = lax.shift_right_logical(col, 3)
+    a = by_three(tap)
+    same = ((col & 7) == (group & 1)) & (tap - 3 * a == b) & (a == xo - (row & 7) + 3)
+    return jnp.where(same, 1.0, 0.0).astype(BF16)
+
+
 def fold_weights(sources, targets, rows):
-    first_order_ref, last_order_ref, first_ref, b1_ref, second_ref, b2_ref, third_ref, b3_ref, last_ref = sources
-    w1_ref, c1_ref, w2_ref, c2_ref, w3_ref, c3_ref, w4_ref = targets
+    first_ref, b1_ref, second_ref, b2_ref, third_ref, b3_ref, last_ref = sources
+    w1_ref, _, w2_ref, c2_ref, w3_ref, c3_ref, w4_ref = targets
     width = second_ref.shape[0]
 
     def padded(ref):
@@ -139,11 +154,19 @@
                 rows[i * inner + j, :count] = ref[i, j].astype(F32)
         return rows[: outer * inner].reshape(outer * inner * 8, width).astype(BF16)
 
-    placed = dot_tn(padded(first_ref), first_order_ref[...])
+    rest = jnp.transpose(jnp.broadcast_to(b1_ref[...] * 0.5, (width, width)))
+    rest = jnp.concatenate([rest, rest], axis=1)
+    lane = lax.broadcasted_iota(jnp.int32, rest.shape, 1)
+    column = jnp.zeros_like(rest)
+    for k in range(3):
+        part = rest.astype(BF16).astype(F32)
+        rest = rest - part
+        column = jnp.where(lane == 240 + k, part, column)
+    placed = dot_tn(padded(first_ref), first_order())
     for xo in range(QUAD):
         moved = pltpu.roll(placed, xo, 1) if xo else placed
-        w1_ref[xo * width : (xo + 1) * width] = moved[:, :240].astype(BF16)
-    placed = dot(last_order_ref[...], padded(last_ref)).astype(BF16)
+        w1_ref[xo * width : (xo + 1) * width] = (moved + column).astype(BF16)
+    placed = dot(last_order(), padded(last_ref)).astype(BF16)
     for xo in range(QUAD):
         w4_ref[:, xo * width : (xo + 1) * width] = placed[xo * 48 : (xo + 1) * 48]
     for source, target in ((second_ref, w2_ref), (third_ref, w3_ref)):
@@ -152,7 +175,7 @@
         target[...] = jnp.concatenate(
             [jnp.concatenate([turned, zeros], axis=1), jnp.concatenate([zeros, turned], axis=1)], axis=0
         )
-    for source, target in ((b1_ref, c1_ref), (b2_ref, c2_ref), (b3_ref, c3_ref)):
+    for source, target in ((b2_ref, c2_ref), (b3_ref, c3_ref)):
         target[...] = jnp.transpose(jnp.broadcast_to(source[...] * 0.5, (width, width)))
 
 
@@ -170,19 +193,20 @@
     return (half + half * jnp.tanh(half)).astype(BF16)
 
 
-def score_kernel(starts, z_count, sources, n_ordered, *refs):
+def score_kernel(spots, sources, n_ordered, *refs):
     refs, out_ref, scratch = refs[:sources], refs[sources + n_ordered], refs[sources + n_ordered + 1 :]
     folded, rows, scratch = scratch[:7], scratch[7], scratch[8:]
     fold_weights(refs[3:], folded, rows)
-    score_slices(starts, z_count, refs[:3], folded, out_ref, *scratch)
-
-
-def score_slices(starts, z_count, planes, weights, out_ref, shifted, windows):
+    score_spots(spots, refs[:3], folded, out_ref, *scratch)
+
+
+def score_spots(spots, planes, weights, out_ref, shifted, windows):
     image_ref, low_ref, high_ref = planes
-    w1_ref, c1_ref, w2_ref, c2_ref, w3_ref, c3_ref, w4_ref = weights
+    w1_ref, w2_ref, c2_ref, w3_ref, c3_ref, w4_ref = weights[:1] + weights[2:]
     slices, _, rows, cols = image_ref.shape
     quads = rows // QUAD
-    width = c1_ref.shape[0]
+    width = c2_ref.shape[0]
+    count = out_ref.shape[0]
     even = lax.axis_index("coil") % 2 == 0
 
     def plane_at(z, p, below_ref, above_ref):
@@ -194,8 +218,8 @@
     def plane(i, p):
         return jnp.where(
             even,
-            plane_at(starts[0] + i - 2, p, high_ref, low_ref),
-            plane_at(starts[1] + i - 2, p, low_ref, high_ref),
+            plane_at(slices - count + i - 2, p, high_ref, low_ref),
+            plane_at(i - 2, p, low_ref, high_ref),
         )
 
     def earlier(values):
@@ -207,7 +231,7 @@
         return jnp.where(at == cols - 1, 0.0, pltpu.roll(values, cols - 1, 1))
 
     shifted[...] = jnp.zeros_like(shifted)
-    for i in range(z_count + 4):
+    for i in range(count + 4):
         for p in range(2):
             values = plane(i, p)
             for b, moved in enumerate((earlier(values), values, later(values))):
@@ -216,19 +240,26 @@
                     start = QUAD * q + 2
                     windows[q, i, b, p * GROUP : (p + 1) * GROUP] = shifted[b, start : start + GROUP].astype(BF16)
 
-    spots = [(q, z) for z in range(z_count) for q in range(quads)]
-    inputs = jnp.concatenate([windows[q, z : z + 5].reshape(240, cols) for q, z in spots], axis=1)
+    place = [jnp.where(even, count - 1 - i, i) for i in range(count)]
+    ones = jnp.ones((16, cols), BF16)
+    inputs = jnp.concatenate(
+        [
+            jnp.concatenate([windows[q, pl.ds(place[i], 5)].reshape(240, cols), ones], axis=0)
+            for i, q in spots
+        ],
+        axis=1,
+    )
     taps = {}
     fields = {}
     row = lax.broadcasted_iota(jnp.int32, (GROUP, cols), 0)
 
-    def add_spot(i):
-        q, z = spots[i]
-        first, last = i * cols, (i + 1) * cols
+    def add_spot(n):
+        i, q = spots[n]
+        first, last = n * cols, (n + 1) * cols
         part = jnp.concatenate(
             [
-                taps[n][:, max(first, n) - n : min(last, n + tile) - n]
-                for n in range(first - first % tile, last, tile)
+                taps[m][:, max(first, m) - m : min(last, m + tile) - m]
+                for m in range(first - first % tile, last, tile)
             ],
             axis=1,
         )
@@ -238,13 +269,15 @@
             moved = pltpu.roll(total[o * GROUP : (o + 1) * GROUP], start % GROUP, 0)
             for t, keep in ((start // GROUP, row >= start % GROUP), (start // GROUP + 1, row < start % GROUP)):
                 if 0 <= t < rows // GROUP:
-                    field = fields.get((z, o, t))
+                    field = fields.get((i, o, t))
                     piece = jnp.where(keep, moved, 0.0)
-                    fields[z, o, t] = piece if field is None else field + piece
-        if q == quads - 1:
+                    fields[i, o, t] = piece if field is None else field + piece
+        if n + 1 == len(spots) or spots[n + 1][0] != i:
             for o in range(2):
                 for t in range(rows // GROUP):
-                    out_ref[z, o, t * GROUP : (t + 1) * GROUP] = fields.pop((z, o, t))
+                    value = fields.pop((i, o, t), None)
+                    value = jnp.zeros((GROUP, cols), F32) if value is None else value
+                    out_ref[place[i], o, t * GROUP : (t + 1) * GROUP] = value
 
     def bias(ref, lanes):
         return jnp.concatenate([jnp.concatenate([ref[...]] * (lanes // 128), axis=1)] * 2, axis=0)
@@ -254,7 +287,7 @@
         lanes = stop - start
         total = dot(w1_ref[half], inputs[:, start:stop])
         yield
-        hidden = half_silu(total + bias(c1_ref, lanes))
+        hidden = half_silu(total)
         yield
         total = dot(w2_ref[...], hidden)
         yield
@@ -277,6 +310,7 @@
     length = len(spots) * cols
     tile = 256
     staggered([chain(n, min(n + tile, length), pair) for n in range(0, length, tile) for pair in range(QUAD // 2)])
+
 
 def adjoint_kernel(
     planes_ref, sens_ref, measured_hbm, mask_ref, half_ref, z_ref, out_ref, y_ref, measured_ref, sems
@@ -379,12 +413,13 @@
     received = back_ref[...].astype(F32).reshape(blocks * block_rows, cols).astype(BF16)
     gradient = dot(order_ref[...], received).reshape(image_ref.shape)
     slices = image_ref.shape[0]
-    cut = one_ref.shape[0]
     even = lax.axis_index("coil") % 2 == 0
     for z in range(slices):
-        at_even = two_ref[z] if z < slices - cut else one_ref[z - (slices - cut)]
-        at_odd = one_ref[z] if z < cut else two_ref[z - cut]
-        field = jnp.where(even, at_even, at_odd)
+        field = two_ref[z]
+        if z == 0:
+            field = field + jnp.where(even, 0.0, one_ref[0])
+        if z == slices - 1:
+            field = field + jnp.where(even, one_ref[0], 0.0)
         out_ref[z] = image_ref[z] + STEP_SIZE * (field - gradient[z]) + noise_ref[z]
 
 
@@ -416,21 +451,19 @@
     low = halo(False, blocks)
     planes = lax.all_to_all(blocks, both, split_axis=0, concat_axis=0, tiled=True)
 
-    cut = max(1, slices // 4)
     weights = (
-        jnp.asarray(first_order()), jnp.asarray(last_order()),
         jnp.transpose(w_first, (0, 2, 1, 3)), b_first[None],
         w_second, b_second[None], w_third, b_third[None], w_last,
     )
 
-    def score(starts, count, flops, planes, *ordered):
+    def score(spots, count, flops, planes, *ordered):
         sources = planes + weights
         return call(
-            lambda *refs: score_kernel(starts, count, len(sources), len(ordered), *refs),
+            lambda *refs: score_kernel(spots, len(sources), len(ordered), *refs),
             jax.ShapeDtypeStruct((count, 2, rows, cols), F32),
             [
-                pltpu.VMEM((QUAD * width, 240), BF16),
-                pltpu.VMEM((width, width), F32),
+                pltpu.VMEM((QUAD * width, 256), BF16),
+                pltpu.VMEM((8, width), F32),
                 pltpu.VMEM((2 * width, 2 * width), BF16),
                 pltpu.VMEM((width, width), F32),
                 pltpu.VMEM((2 * width, 2 * width), BF16),
@@ -445,9 +478,11 @@
             in_specs=[VMEM] * len(sources) + [pl.BlockSpec(memory_space=pl.ANY)] * len(ordered),
         )(*sources, *ordered)
 
-    apart = slices - cut >= 2
+    spots = [(i, q) for i in range(slices) for q in range(rows // QUAD)]
+    early = rows // QUAD * EARLY // 4
+    apart = slices >= 3
     high = None if apart else halo(True, blocks)
-    score_one = score((slices - cut, 0), cut, SHORT, (image, low, low if apart else high))
+    score_one = score(spots[:early], 1, SHORT, (image, low, low if apart else high))
     if apart:
         high = halo(True, score_one)
     z_tables = np.concatenate([dft_table(depth).T, depth_order(devices, x_local, slices)], axis=0)
@@ -456,7 +491,7 @@
          pltpu.SemaphoreType.DMA((sens.shape[0],))],
         flops=BUSY, nbytes=5 * 10**6, limit=WIDE_LIMIT, in_specs=[VMEM] * 2 + [HBM] + [VMEM] * 3
     )(planes, sens, measured, mask, jnp.asarray(dft_table(cols)[:cols]), jnp.asarray(z_tables))
-    score_two = score((0, cut), slices - cut, BUSY, (image, low, high), partial)
+    score_two = score(spots[early:], slices, BUSY, (image, low, high), partial)
     back = lax.all_to_all(partial, both, split_axis=0, concat_axis=0, tiled=True)
     return call(final_kernel, jax.ShapeDtypeStruct(image.shape, F32), nbytes=10**6)(
         image, noise, score_one, score_two, back,

time: 36.6 us -> 36.6 us (level)
  local copies, waits for them, and re-layouts: 1.97 us -> 1.01 us
  waiting for transfers between devices: 4.29 us -> 4.9 us
  Pallas kernels: 16.3 us -> 16.7 us
    all_to_all x1, waiting for transfers between devices: 2.76 us -> 3.72 us  [on_device(): lax.all_to_all(blocks, both, split_axis=0, concat_axis=0, tiled=True)]
    unnamed x36 -> x30, local copies, waits for them, and re-layouts: 1.97 us -> 1.01 us
    pallas_call x2, Pallas kernels: 9.16 us -> 9.53 us  [score(): call(lambda *refs: score_kernel(spots, len(sources), len(ordered), *refs)...]
  transfers between devices with their start and end apart: 4 -> 4, of which waited for: 2 -> 2; matrix products, arithmetic and copies ran while one was open for 0% -> 0% of each run, Pallas kernels for 40% -> 41%
where the time goes in v2:
time: 36.6 us; the launch traced here: 36.3 us
  Pallas kernels  16.7 us (46%)
  starting transfers between devices  13.5 us (37%)
  waiting for transfers between devices  4.9 us (13%)
  local copies, waits for them, and re-layouts  1.01 us (3%)
    pallas_call x2, Pallas kernels, score(): call(lambda *refs: score_kernel(spots, len(sources), len(ordered), *refs)...  9.53 us
    all_to_all x1, starting transfers between devices, on_device(): lax.all_to_all(blocks, both, split_axis=0, concat_axis=0, tiled=True)  7.15 us
    pallas_call x1, Pallas kernels, on_device(): call(adjoint_kernel, block, [pltpu.VMEM((2 * cols, 2 * cols), BF16), pltp...  5.39 us
    ppermute x2, starting transfers between devices, halo(): return lax.ppermute(slab, both, across if outward else pairs)  3.8 us
    all_to_all x1, waiting for transfers between devices, on_device(): lax.all_to_all(blocks, both, split_axis=0, concat_axis=0, tiled=True)  3.72 us
    all_to_all x1, starting transfers between devices, on_device(): lax.all_to_all(partial, both, split_axis=0, concat_axis=0, tiled=True)  2.52 us
    all_to_all x1, waiting for transfers between devices, on_device(): lax.all_to_all(partial, both, split_axis=0, concat_axis=0, tiled=True)  1.17 us
    unnamed x30, local copies, waits for them, and re-layouts  1.01 us
  transfers between devices with their start and end apart: 4, of which 2 were waited for; matrix products, arithmetic and copies ran while one was open for 0% of the time, Pallas kernels for 41%

profile of v2, /device:TPU:1, one launch (start us, length us, event | category | flops | bytes accessed | tf_op | source)
XLA Modules:
  0.0 36.3 jit_solution(7578510596262913773)
XLA Ops:
  0.0 0.9 %copy-done = f32[4,2,16,384]{3,2,1,0:T(8,128)S(1)} copy-done((f32[4,2,16,384]{3,2,1,0:T(8,128)S(1)}, f32[4,2,16,384]{3,2,1,0:T(8,128)}, u32[]{:S(2)}) %copy-start) | copy-done | bytes 196632
  0.9 0.8 %shard_map.145.after_ref = bf16[32,8,384]{2,1,0:T(8,128)(2,1)} custom-call(f32[4,2,16,384]{3,2,1,0:T(8,128)S(1)} %copy-done), custom_call_target="tpu_custom_call" | custom-call | flops 40000000000 | bytes 1000000 | tf_op jit(solution)/shard_map/pallas_call | solution.py:439
  1.8 0.0 copy-start.9
  1.8 0.0 copy-start.10
  1.8 0.0 copy-start.11
  1.8 0.0 copy-start.12
  1.9 0.1 collective-permute-start
  2.0 7.2 %all-to-all-start = ((bf16[32,8,384]{2,1,0:T(8,128)(2,1)}), bf16[32,8,384]{2,1,0:T(8,128)(2,1)S(1)}, u32[]{:S(2)}, u32[]{:S(2)}) async-start(bf16[32,8,384]{2,1,0:T(8,128)(2,1)} %shard_map.145.after_ref), calls=%async_computation | async-start | bytes 393216 | tf_op jit(solution)/shard_map/all_to_all | solution.py:452
  9.2 0.0 collective-permute-done.refs_1_.refs_2_
  9.2 1.6 %shard_map.147.after_ref.one_ref = f32[1,2,16,384]{3,2,1,0:T(8,128)S(1)} custom-call(f32[4,2,16,384]{3,2,1,0:T(8,128)S(1)} %copy-done.1, bf16[2,2,16,384]{3,2,1,0:T(8,128)(2,1)S(1)} %collective-permute-done.refs_1_.refs_2_, bf16[2,2,16,384]{3,2,1,0:T(8,128)(2,1)S(1)} %collective-permute-done.refs_1_.refs_2_, bf16[3,10,3,128]{3,2,1,0:T(4,128)(2,1)S(1)} %bitcast.4, ...), custom_call_target="tpu_custom_call" | custom-call | flops 40000000000 | bytes 2000000 | tf_op jit(solution)/shard_map/pallas_call | solution.py:461
  10.9 0.0 copy-start.4
  10.9 0.0 copy-start.5
  10.9 0.0 copy-start.13
  10.9 0.0 copy-start.14
  11.0 3.7 %collective-permute-start.1 = (bf16[2,2,16,384]{3,2,1,0:T(8,128)(2,1)S(1)}, bf16[2,2,16,384]{3,2,1,0:T(8,128)(2,1)S(1)}, u32[]{:S(2)}, u32[]{:S(2)}) collective-permute-start(bf16[2,2,16,384]{3,2,1,0:T(8,128)(2,1)S(1)} %shard_map.148), channel_id=1, source_target_pairs={{1,2},{2,1},{3,4},{4,3},{5,6},{6,5},{7,8},{8,7},{9,10},{10,9},{11,... | collective-permute-start | bytes 147464 | tf_op jit(solution)/shard_map/ppermute | solution.py:449
  14.7 3.7 %all-to-all-done.planes_ref = bf16[32,8,384]{2,1,0:T(8,128)(2,1)S(1)} async-done(((bf16[32,8,384]{2,1,0:T(8,128)(2,1)}), bf16[32,8,384]{2,1,0:T(8,128)(2,1)S(1)}, u32[]{:S(2)}, u32[]{:S(2)}) %all-to-all-start) | async-done | bytes 196640 | tf_op jit(solution)/shard_map/all_to_all | solution.py:452
  18.4 5.4 %shard_map.149.refs_10_ = bf16[32,8,384]{2,1,0:T(8,128)(2,1)} custom-call(bf16[32,8,384]{2,1,0:T(8,128)(2,1)S(1)} %all-to-all-done.planes_ref, bf16[8,2,1,384,128]{4,3,2,1,0:T(8,128)(2,1)S(1)} %copy-done.4, bf16[8,2,1,384,128]{4,3,2,1,0:T(8,128)(2,1)} %measured_hbm.1, s32[384,128]{1,0:T(8,128)S(1)} %copy-done.5, bf16[384,768]{1,0:T(8,128)(2,1)S(1)} %copy-done.13, ...), custom_call_target="tpu_custom_call" | custom-call | flops 40000000000 | bytes 5000000 | tf_op jit(solution)/shard_map/pallas_call | solution.py:489
  23.8 2.5 %all-to-all-start.1 = ((bf16[32,8,384]{2,1,0:T(8,128)(2,1)}), bf16[32,8,384]{2,1,0:T(8,128)(2,1)S(1)}, u32[]{:S(2)}, u32[]{:S(2)}) async-start(bf16[32,8,384]{2,1,0:T(8,128)(2,1)} %shard_map.149.refs_10_), calls=%async_computation.1 | async-start | bytes 393216 | tf_op jit(solution)/shard_map/all_to_all | solution.py:495
  26.3 0.0 copy-start.2
  26.3 0.0 copy-start.3
  26.3 0.0 collective-permute-done.1.refs_2_
  26.4 7.9 %shard_map.150.two_ref = f32[4,2,16,384]{3,2,1,0:T(8,128)S(1)} custom-call(f32[4,2,16,384]{3,2,1,0:T(8,128)S(1)} %copy-done.1, bf16[2,2,16,384]{3,2,1,0:T(8,128)(2,1)S(1)} %collective-permute-done.refs_1_.refs_2_, bf16[2,2,16,384]{3,2,1,0:T(8,128)(2,1)S(1)} %collective-permute-done.1.refs_2_, bf16[3,10,3,128]{3,2,1,0:T(4,128)(2,1)S(1)} %bitcast.5, ...), custom_call_target="tpu_custom_call" | custom-call | flops 40000000000 | bytes 2000000 | tf_op jit(solution)/shard_map/pallas_call | solution.py:461
  34.2 1.2 %all-to-all-done.1.back_ref = bf16[32,8,384]{2,1,0:T(8,128)(2,1)S(1)} async-done(((bf16[32,8,384]{2,1,0:T(8,128)(2,1)}), bf16[32,8,384]{2,1,0:T(8,128)(2,1)S(1)}, u32[]{:S(2)}, u32[]{:S(2)}) %all-to-all-start.1) | async-done | bytes 196640 | tf_op jit(solution)/shard_map/all_to_all | solution.py:495
  35.4 0.9 %shard_map.151 = f32[4,2,16,384]{3,2,1,0:T(8,128)} custom-call(f32[4,2,16,384]{3,2,1,0:T(8,128)S(1)} %copy-done.1, f32[4,2,16,384]{3,2,1,0:T(8,128)S(1)} %copy-done.2, f32[1,2,16,384]{3,2,1,0:T(8,128)S(1)} %shard_map.147.after_ref.one_ref, f32[4,2,16,384]{3,2,1,0:T(8,128)S(1)} %shard_map.150.two_ref, bf16[32,8,384]{2,1,0:T(8,128)(2,1)S(1)} %all-to-all-done.1.back_ref, ...), custom_call_target="tpu_custom_call" | custom-call | bytes 1000000 | tf_op jit(solution)/shard_map/pallas_call | solution.py:496
  (21 shorter events, 0.1 us)
Async XLA Ops:
  0.0 0.9 %copy-start = (f32[4,2,16,384]{3,2,1,0:T(8,128)S(1)}, f32[4,2,16,384]{3,2,1,0:T(8,128)}, u32[]{:S(2)}) copy-start(f32[4,2,16,384]{3,2,1,0:T(8,128)} %image_ref.7) | copy-start | bytes 589828
  1.8 7.4 %copy-start.1 = (f32[4,2,16,384]{3,2,1,0:T(8,128)S(1)}, f32[4,2,16,384]{3,2,1,0:T(8,128)}, u32[]{:S(2)}) copy-start(f32[4,2,16,384]{3,2,1,0:T(8,128)} %image_ref.7) | copy-start | bytes 589828
  1.8 7.4 %copy-start.6 = (bf16[128,128]{1,0:T(8,128)(2,1)S(1)}, bf16[128,128]{1,0:T(8,128)(2,1)}, u32[]{:S(2)}) copy-start(bf16[128,128]{1,0:T(8,128)(2,1)} %refs_5_.3) | copy-start | bytes 98308
  1.8 7.4 %copy-start.7 = (bf16[128,128]{1,0:T(8,128)(2,1)S(1)}, bf16[128,128]{1,0:T(8,128)(2,1)}, u32[]{:S(2)}) copy-start(bf16[128,128]{1,0:T(8,128)(2,1)} %refs_7_.3) | copy-start | bytes 98308
  1.8 7.4 %copy-start.8 = (bf16[3,3,10,128]{3,1,2,0:T(4,128)(2,1)S(1)}, bf16[3,3,10,128]{3,1,2,0:T(4,128)(2,1)}, u32[]{:S(2)}) copy-start(bf16[3,3,10,128]{3,1,2,0:T(4,128)(2,1)} %param.20) | copy-start | bytes 69124
  1.8 7.4 %copy-start.9 = (bf16[3,3,2,128]{3,2,1,0:T(2,128)(2,1)S(1)}, bf16[3,3,2,128]{3,2,1,0:T(2,128)(2,1)}, u32[]{:S(2)}) copy-start(bf16[3,3,2,128]{3,2,1,0:T(2,128)(2,1)} %refs_9_.3) | copy-start | bytes 13828
  1.8 7.4 %copy-start.10 = (f32[128]{0:T(128)S(1)}, f32[128]{0:T(128)}, u32[]{:S(2)}) copy-start(f32[128]{0:T(128)} %param.21) | copy-start | bytes 1540
  1.8 7.4 %copy-start.11 = (f32[128]{0:T(128)S(1)}, f32[128]{0:T(128)}, u32[]{:S(2)}) copy-start(f32[128]{0:T(128)} %param.23) | copy-start | bytes 1540
  1.8 7.4 %copy-start.12 = (f32[128]{0:T(128)S(1)}, f32[128]{0:T(128)}, u32[]{:S(2)}) copy-start(f32[128]{0:T(128)} %param.25) | copy-start | bytes 1540
  1.9 7.3 %collective-permute-start = (bf16[2,2,16,384]{3,2,1,0:T(8,128)(2,1)S(1)}, bf16[2,2,16,384]{3,2,1,0:T(8,128)(2,1)S(1)}, u32[]{:S(2)}, u32[]{:S(2)}) collective-permute-start(bf16[2,2,16,384]{3,2,1,0:T(8,128)(2,1)S(1)} %shard_map.146), channel_id=1, source_target_pairs={{0,1},{1,0},{2,3},{3,2},{4,5},{5,4},{6,7},{7,6},{8,9},{9,8},{10,11... | collective-permute-start | bytes 147464 | tf_op jit(solution)/shard_map/ppermute | solution.py:449
  2.0 16.4 %all-to-all-start = ((bf16[32,8,384]{2,1,0:T(8,128)(2,1)}), bf16[32,8,384]{2,1,0:T(8,128)(2,1)S(1)}, u32[]{:S(2)}, u32[]{:S(2)}) async-start(bf16[32,8,384]{2,1,0:T(8,128)(2,1)} %shard_map.145.after_ref), calls=%async_computation | async-start | bytes 393216 | tf_op jit(solution)/shard_map/all_to_all | solution.py:452
  10.9 7.5 %copy-start.4 = (bf16[8,2,1,384,128]{4,3,2,1,0:T(8,128)(2,1)S(1)}, bf16[8,2,1,384,128]{4,3,2,1,0:T(8,128)(2,1)}, u32[]{:S(2)}) copy-start(bf16[8,2,1,384,128]{4,3,2,1,0:T(8,128)(2,1)} %sens_ref.1) | copy-start | bytes 4718596
  10.9 7.5 %copy-start.5 = (s32[384,128]{1,0:T(8,128)S(1)}, s32[384,128]{1,0:T(8,128)}, u32[]{:S(2)}) copy-start(s32[384,128]{1,0:T(8,128)} %mask_ref.1) | copy-start | bytes 589828
  10.9 7.5 %copy-start.13 = (bf16[384,768]{1,0:T(8,128)(2,1)S(1)}, bf16[384,768]{1,0:T(8,128)(2,1)}, u32[]{:S(2)}) copy-start(bf16[384,768]{1,0:T(8,128)(2,1)} %constant.6.clone.half_ref) | copy-start | bytes 1769476
  10.9 7.5 %copy-start.14 = (bf16[512,256]{1,0:T(8,128)(2,1)S(1)}, bf16[512,256]{1,0:T(8,128)(2,1)}, u32[]{:S(2)}) copy-start(bf16[512,256]{1,0:T(8,128)(2,1)} %constant.7.clone.z_ref) | copy-start | bytes 786436
  11.0 15.4 %collective-permute-start.1 = (bf16[2,2,16,384]{3,2,1,0:T(8,128)(2,1)S(1)}, bf16[2,2,16,384]{3,2,1,0:T(8,128)(2,1)S(1)}, u32[]{:S(2)}, u32[]{:S(2)}) collective-permute-start(bf16[2,2,16,384]{3,2,1,0:T(8,128)(2,1)S(1)} %shard_map.148), channel_id=1, source_target_pairs={{1,2},{2,1},{3,4},{4,3},{5,6},{6,5},{7,8},{8,7},{9,10},{10,9},{11,... | collective-permute-start | bytes 147464 | tf_op jit(solution)/shard_map/ppermute | solution.py:449
  23.8 11.6 %all-to-all-start.1 = ((bf16[32,8,384]{2,1,0:T(8,128)(2,1)}), bf16[32,8,384]{2,1,0:T(8,128)(2,1)S(1)}, u32[]{:S(2)}, u32[]{:S(2)}) async-start(bf16[32,8,384]{2,1,0:T(8,128)(2,1)} %shard_map.149.refs_10_), calls=%async_computation.1 | async-start | bytes 393216 | tf_op jit(solution)/shard_map/all_to_all | solution.py:495
  26.3 9.1 %copy-start.2 = (f32[4,2,16,384]{3,2,1,0:T(8,128)S(1)}, f32[4,2,16,384]{3,2,1,0:T(8,128)}, u32[]{:S(2)}) copy-start(f32[4,2,16,384]{3,2,1,0:T(8,128)} %noise_ref.1) | copy-start | bytes 589828
  26.3 9.1 %copy-start.3 = (bf16[128,256]{1,0:T(8,128)(2,1)S(1)}, bf16[128,256]{1,0:T(8,128)(2,1)}, u32[]{:S(2)}) copy-start(bf16[128,256]{1,0:T(8,128)(2,1)} %constant.8.clone.order_ref) | copy-start | bytes 196612

commit v3 on v2

--- a/solution.py
+++ b/solution.py
@@ -194,13 +194,14 @@
 
 
 def score_kernel(spots, sources, n_ordered, *refs):
+    added = refs[sources : sources + n_ordered - 1]
     refs, out_ref, scratch = refs[:sources], refs[sources + n_ordered], refs[sources + n_ordered + 1 :]
     folded, rows, scratch = scratch[:7], scratch[7], scratch[8:]
     fold_weights(refs[3:], folded, rows)
-    score_spots(spots, refs[:3], folded, out_ref, *scratch)
-
-
-def score_spots(spots, planes, weights, out_ref, shifted, windows):
+    score_spots(spots, refs[:3], folded, added, out_ref, *scratch)
+
+
+def score_spots(spots, planes, weights, added, out_ref, shifted, windows):
     image_ref, low_ref, high_ref = planes
     w1_ref, w2_ref, c2_ref, w3_ref, c3_ref, w4_ref = weights[:1] + weights[2:]
     slices, _, rows, cols = image_ref.shape
@@ -277,7 +278,13 @@
                 for t in range(rows // GROUP):
                     value = fields.pop((i, o, t), None)
                     value = jnp.zeros((GROUP, cols), F32) if value is None else value
-                    out_ref[place[i], o, t * GROUP : (t + 1) * GROUP] = value
+                    at = (place[i], o, slice(t * GROUP, (t + 1) * GROUP))
+                    if added:
+                        noise_ref, one_ref = added
+                        if i == 0:
+                            value = value + one_ref[0, o, at[2]]
+                        value = image_ref[at] + STEP_SIZE * value + noise_ref[at]
+                    out_ref[at] = value
 
     def bias(ref, lanes):
         return jnp.concatenate([jnp.concatenate([ref[...]] * (lanes // 128), axis=1)] * 2, axis=0)
@@ -408,19 +415,11 @@
     out_ref[...] = result.reshape(out_ref.shape).astype(BF16)
 
 
-def final_kernel(image_ref, noise_ref, one_ref, two_ref, back_ref, order_ref, out_ref):
+def final_kernel(moved_ref, back_ref, order_ref, out_ref):
     blocks, block_rows, cols = back_ref.shape
     received = back_ref[...].astype(F32).reshape(blocks * block_rows, cols).astype(BF16)
-    gradient = dot(order_ref[...], received).reshape(image_ref.shape)
-    slices = image_ref.shape[0]
-    even = lax.axis_index("coil") % 2 == 0
-    for z in range(slices):
-        field = two_ref[z]
-        if z == 0:
-            field = field + jnp.where(even, 0.0, one_ref[0])
-        if z == slices - 1:
-            field = field + jnp.where(even, one_ref[0], 0.0)
-        out_ref[z] = image_ref[z] + STEP_SIZE * (field - gradient[z]) + noise_ref[z]
+    gradient = dot(order_ref[...], received).reshape(moved_ref.shape)
+    out_ref[...] = moved_ref[...] - STEP_SIZE * gradient
 
 
 def on_device(
@@ -475,7 +474,8 @@
             ],
             flops=flops,
             nbytes=2 * 10**6,
-            in_specs=[VMEM] * len(sources) + [pl.BlockSpec(memory_space=pl.ANY)] * len(ordered),
+            in_specs=[VMEM] * (len(sources) + max(0, len(ordered) - 1))
+            + [pl.BlockSpec(memory_space=pl.ANY)] * min(1, len(ordered)),
         )(*sources, *ordered)
 
     spots = [(i, q) for i in range(slices) for q in range(rows // QUAD)]
@@ -491,10 +491,10 @@
          pltpu.SemaphoreType.DMA((sens.shape[0],))],
         flops=BUSY, nbytes=5 * 10**6, limit=WIDE_LIMIT, in_specs=[VMEM] * 2 + [HBM] + [VMEM] * 3
     )(planes, sens, measured, mask, jnp.asarray(dft_table(cols)[:cols]), jnp.asarray(z_tables))
-    score_two = score(spots[early:], slices, BUSY, (image, low, high), partial)
+    moved = score(spots[early:], slices, BUSY, (image, low, high), noise, score_one, partial)
     back = lax.all_to_all(partial, both, split_axis=0, concat_axis=0, tiled=True)
     return call(final_kernel, jax.ShapeDtypeStruct(image.shape, F32), nbytes=10**6)(
-        image, noise, score_one, score_two, back,
+        moved, back,
         jnp.asarray(gather_order(slabs, groups, x_local, slices)),
     )
 

time: 36.6 us -> 36.6 us (level)
  no operation moved by 1% of the time
where the time goes in v3:
time: 36.6 us; the launch traced here: 36.3 us
  Pallas kernels  16.7 us (46%)
  starting transfers between devices  13.5 us (37%)
  waiting for transfers between devices  4.89 us (13%)
  local copies, waits for them, and re-layouts  1.01 us (3%)
    pallas_call x2, Pallas kernels, score(): call(lambda *refs: score_kernel(spots, len(sources), len(ordered), *refs)...  9.52 us
    all_to_all x1, starting transfers between devices, on_device(): lax.all_to_all(blocks, both, split_axis=0, concat_axis=0, tiled=True)  7.15 us
    pallas_call x1, Pallas kernels, on_device(): call(adjoint_kernel, block, [pltpu.VMEM((2 * cols, 2 * cols), BF16), pltp...  5.39 us
    ppermute x2, starting transfers between devices, halo(): return lax.ppermute(slab, both, across if outward else pairs)  3.8 us
    all_to_all x1, waiting for transfers between devices, on_device(): lax.all_to_all(blocks, both, split_axis=0, concat_axis=0, tiled=True)  3.71 us
    all_to_all x1, starting transfers between devices, on_device(): lax.all_to_all(partial, both, split_axis=0, concat_axis=0, tiled=True)  2.52 us
    all_to_all x1, waiting for transfers between devices, on_device(): lax.all_to_all(partial, both, split_axis=0, concat_axis=0, tiled=True)  1.17 us
    unnamed x30, local copies, waits for them, and re-layouts  1.01 us
  transfers between devices with their start and end apart: 4, of which 2 were waited for; matrix products, arithmetic and copies ran while one was open for 0% of the time, Pallas kernels for 41%

profile of v3, /device:TPU:1, one launch (start us, length us, event | category | flops | bytes accessed | tf_op | source)
XLA Modules:
  0.0 36.3 jit_solution(3993772685879120454)
XLA Ops:
  0.0 0.9 %copy-done.3 = f32[4,2,16,384]{3,2,1,0:T(8,128)S(1)} copy-done((f32[4,2,16,384]{3,2,1,0:T(8,128)S(1)}, f32[4,2,16,384]{3,2,1,0:T(8,128)}, u32[]{:S(2)}) %copy-start.3) | copy-done | bytes 196632
  0.9 0.8 %shard_map.145.after_ref = bf16[32,8,384]{2,1,0:T(8,128)(2,1)} custom-call(f32[4,2,16,384]{3,2,1,0:T(8,128)S(1)} %copy-done.3), custom_call_target="tpu_custom_call" | custom-call | flops 40000000000 | bytes 1000000 | tf_op jit(solution)/shard_map/pallas_call | solution.py:438
  1.8 0.0 copy-start.9
  1.8 0.0 copy-start.10
  1.8 0.0 copy-start.11
  1.8 0.0 copy-start.12
  1.9 0.1 collective-permute-start
  2.0 7.2 %all-to-all-start = ((bf16[32,8,384]{2,1,0:T(8,128)(2,1)}), bf16[32,8,384]{2,1,0:T(8,128)(2,1)S(1)}, u32[]{:S(2)}, u32[]{:S(2)}) async-start(bf16[32,8,384]{2,1,0:T(8,128)(2,1)} %shard_map.145.after_ref), calls=%async_computation | async-start | bytes 393216 | tf_op jit(solution)/shard_map/all_to_all | solution.py:451
  9.2 0.0 collective-permute-done.refs_1_.refs_2_
  9.2 1.6 %shard_map.147.after_ref.refs_11_ = f32[1,2,16,384]{3,2,1,0:T(8,128)S(1)} custom-call(f32[4,2,16,384]{3,2,1,0:T(8,128)S(1)} %copy-done.4, bf16[2,2,16,384]{3,2,1,0:T(8,128)(2,1)S(1)} %collective-permute-done.refs_1_.refs_2_, bf16[2,2,16,384]{3,2,1,0:T(8,128)(2,1)S(1)} %collective-permute-done.refs_1_.refs_2_, bf16[3,10,3,128]{3,2,1,0:T(4,128)(2,1)S(1)} %bitcast.4, ...), custom_call_target="tpu_custom_call" | custom-call | flops 40000000000 | bytes 2000000 | tf_op jit(solution)/shard_map/pallas_call | solution.py:460
  10.9 0.0 copy-start.1
  10.9 0.0 copy-start.2
  10.9 0.0 copy-start.13
  10.9 0.0 copy-start.14
  11.0 0.0 copy-start.5
  11.0 3.7 %collective-permute-start.1 = (bf16[2,2,16,384]{3,2,1,0:T(8,128)(2,1)S(1)}, bf16[2,2,16,384]{3,2,1,0:T(8,128)(2,1)S(1)}, u32[]{:S(2)}, u32[]{:S(2)}) collective-permute-start(bf16[2,2,16,384]{3,2,1,0:T(8,128)(2,1)S(1)} %shard_map.148), channel_id=1, source_target_pairs={{1,2},{2,1},{3,4},{4,3},{5,6},{6,5},{7,8},{8,7},{9,10},{10,9},{11,... | collective-permute-start | bytes 147464 | tf_op jit(solution)/shard_map/ppermute | solution.py:448
  14.7 3.7 %all-to-all-done.planes_ref = bf16[32,8,384]{2,1,0:T(8,128)(2,1)S(1)} async-done(((bf16[32,8,384]{2,1,0:T(8,128)(2,1)}), bf16[32,8,384]{2,1,0:T(8,128)(2,1)S(1)}, u32[]{:S(2)}, u32[]{:S(2)}) %all-to-all-start) | async-done | bytes 196640 | tf_op jit(solution)/shard_map/all_to_all | solution.py:451
  18.4 5.4 %shard_map.149.refs_12_ = bf16[32,8,384]{2,1,0:T(8,128)(2,1)} custom-call(bf16[32,8,384]{2,1,0:T(8,128)(2,1)S(1)} %all-to-all-done.planes_ref, bf16[8,2,1,384,128]{4,3,2,1,0:T(8,128)(2,1)S(1)} %copy-done.1, bf16[8,2,1,384,128]{4,3,2,1,0:T(8,128)(2,1)} %measured_hbm.1, s32[384,128]{1,0:T(8,128)S(1)} %copy-done.2, bf16[384,768]{1,0:T(8,128)(2,1)S(1)} %copy-done.13, ...), custom_call_target="tpu_custom_call" | custom-call | flops 40000000000 | bytes 5000000 | tf_op jit(solution)/shard_map/pallas_call | solution.py:489
  23.8 2.5 %all-to-all-start.1 = ((bf16[32,8,384]{2,1,0:T(8,128)(2,1)}), bf16[32,8,384]{2,1,0:T(8,128)(2,1)S(1)}, u32[]{:S(2)}, u32[]{:S(2)}) async-start(bf16[32,8,384]{2,1,0:T(8,128)(2,1)} %shard_map.149.refs_12_), calls=%async_computation.1 | async-start | bytes 393216 | tf_op jit(solution)/shard_map/all_to_all | solution.py:495
  26.3 0.0 copy-start
  26.3 0.0 collective-permute-done.1.refs_2_
  26.4 7.9 %shard_map.150.moved_ref = f32[4,2,16,384]{3,2,1,0:T(8,128)S(1)} custom-call(f32[4,2,16,384]{3,2,1,0:T(8,128)S(1)} %copy-done.4, bf16[2,2,16,384]{3,2,1,0:T(8,128)(2,1)S(1)} %collective-permute-done.refs_1_.refs_2_, bf16[2,2,16,384]{3,2,1,0:T(8,128)(2,1)S(1)} %collective-permute-done.1.refs_2_, bf16[3,10,3,128]{3,2,1,0:T(4,128)(2,1)S(1)} %bitcast.5, ...), custom_call_target="tpu_custom_call" | custom-call | flops 40000000000 | bytes 2000000 | tf_op jit(solution)/shard_map/pallas_call | solution.py:460
  34.2 1.2 %all-to-all-done.1.back_ref = bf16[32,8,384]{2,1,0:T(8,128)(2,1)S(1)} async-done(((bf16[32,8,384]{2,1,0:T(8,128)(2,1)}), bf16[32,8,384]{2,1,0:T(8,128)(2,1)S(1)}, u32[]{:S(2)}, u32[]{:S(2)}) %all-to-all-start.1) | async-done | bytes 196640 | tf_op jit(solution)/shard_map/all_to_all | solution.py:495
  35.4 0.9 %shard_map.151 = f32[4,2,16,384]{3,2,1,0:T(8,128)} custom-call(f32[4,2,16,384]{3,2,1,0:T(8,128)S(1)} %shard_map.150.moved_ref, bf16[32,8,384]{2,1,0:T(8,128)(2,1)S(1)} %all-to-all-done.1.back_ref, bf16[128,256]{1,0:T(8,128)(2,1)S(1)} %copy-done), custom_call_target="tpu_custom_call" | custom-call | bytes 1000000 | tf_op jit(solution)/shard_map/pallas_call | solution.py:496
  (21 shorter events, 0.1 us)
Async XLA Ops:
  0.0 0.9 %copy-start.3 = (f32[4,2,16,384]{3,2,1,0:T(8,128)S(1)}, f32[4,2,16,384]{3,2,1,0:T(8,128)}, u32[]{:S(2)}) copy-start(f32[4,2,16,384]{3,2,1,0:T(8,128)} %refs_0_.3) | copy-start | bytes 589828
  1.8 7.4 %copy-start.4 = (f32[4,2,16,384]{3,2,1,0:T(8,128)S(1)}, f32[4,2,16,384]{3,2,1,0:T(8,128)}, u32[]{:S(2)}) copy-start(f32[4,2,16,384]{3,2,1,0:T(8,128)} %refs_0_.3) | copy-start | bytes 589828
  1.8 7.4 %copy-start.6 = (bf16[128,128]{1,0:T(8,128)(2,1)S(1)}, bf16[128,128]{1,0:T(8,128)(2,1)}, u32[]{:S(2)}) copy-start(bf16[128,128]{1,0:T(8,128)(2,1)} %refs_5_.3) | copy-start | bytes 98308
  1.8 7.4 %copy-start.7 = (bf16[128,128]{1,0:T(8,128)(2,1)S(1)}, bf16[128,128]{1,0:T(8,128)(2,1)}, u32[]{:S(2)}) copy-start(bf16[128,128]{1,0:T(8,128)(2,1)} %refs_7_.3) | copy-start | bytes 98308
  1.8 7.4 %copy-start.8 = (bf16[3,3,10,128]{3,1,2,0:T(4,128)(2,1)S(1)}, bf16[3,3,10,128]{3,1,2,0:T(4,128)(2,1)}, u32[]{:S(2)}) copy-start(bf16[3,3,10,128]{3,1,2,0:T(4,128)(2,1)} %param.20) | copy-start | bytes 69124
  1.8 7.4 %copy-start.9 = (bf16[3,3,2,128]{3,2,1,0:T(2,128)(2,1)S(1)}, bf16[3,3,2,128]{3,2,1,0:T(2,128)(2,1)}, u32[]{:S(2)}) copy-start(bf16[3,3,2,128]{3,2,1,0:T(2,128)(2,1)} %refs_9_.3) | copy-start | bytes 13828
  1.8 7.4 %copy-start.10 = (f32[128]{0:T(128)S(1)}, f32[128]{0:T(128)}, u32[]{:S(2)}) copy-start(f32[128]{0:T(128)} %param.21) | copy-start | bytes 1540
  1.8 7.4 %copy-start.11 = (f32[128]{0:T(128)S(1)}, f32[128]{0:T(128)}, u32[]{:S(2)}) copy-start(f32[128]{0:T(128)} %param.23) | copy-start | bytes 1540
  1.8 7.4 %copy-start.12 = (f32[128]{0:T(128)S(1)}, f32[128]{0:T(128)}, u32[]{:S(2)}) copy-start(f32[128]{0:T(128)} %param.25) | copy-start | bytes 1540
  1.9 7.3 %collective-permute-start = (bf16[2,2,16,384]{3,2,1,0:T(8,128)(2,1)S(1)}, bf16[2,2,16,384]{3,2,1,0:T(8,128)(2,1)S(1)}, u32[]{:S(2)}, u32[]{:S(2)}) collective-permute-start(bf16[2,2,16,384]{3,2,1,0:T(8,128)(2,1)S(1)} %shard_map.146), channel_id=1, source_target_pairs={{0,1},{1,0},{2,3},{3,2},{4,5},{5,4},{6,7},{7,6},{8,9},{9,8},{10,11... | collective-permute-start | bytes 147464 | tf_op jit(solution)/shard_map/ppermute | solution.py:448
  2.0 16.4 %all-to-all-start = ((bf16[32,8,384]{2,1,0:T(8,128)(2,1)}), bf16[32,8,384]{2,1,0:T(8,128)(2,1)S(1)}, u32[]{:S(2)}, u32[]{:S(2)}) async-start(bf16[32,8,384]{2,1,0:T(8,128)(2,1)} %shard_map.145.after_ref), calls=%async_computation | async-start | bytes 393216 | tf_op jit(solution)/shard_map/all_to_all | solution.py:451
  10.9 7.5 %copy-start.1 = (bf16[8,2,1,384,128]{4,3,2,1,0:T(8,128)(2,1)S(1)}, bf16[8,2,1,384,128]{4,3,2,1,0:T(8,128)(2,1)}, u32[]{:S(2)}) copy-start(bf16[8,2,1,384,128]{4,3,2,1,0:T(8,128)(2,1)} %sens_ref.1) | copy-start | bytes 4718596
  10.9 7.5 %copy-start.2 = (s32[384,128]{1,0:T(8,128)S(1)}, s32[384,128]{1,0:T(8,128)}, u32[]{:S(2)}) copy-start(s32[384,128]{1,0:T(8,128)} %mask_ref.1) | copy-start | bytes 589828
  10.9 7.5 %copy-start.13 = (bf16[384,768]{1,0:T(8,128)(2,1)S(1)}, bf16[384,768]{1,0:T(8,128)(2,1)}, u32[]{:S(2)}) copy-start(bf16[384,768]{1,0:T(8,128)(2,1)} %constant.6.clone.half_ref) | copy-start | bytes 1769476
  10.9 7.5 %copy-start.14 = (bf16[512,256]{1,0:T(8,128)(2,1)S(1)}, bf16[512,256]{1,0:T(8,128)(2,1)}, u32[]{:S(2)}) copy-start(bf16[512,256]{1,0:T(8,128)(2,1)} %constant.7.clone.z_ref) | copy-start | bytes 786436
  11.0 15.4 %copy-start.5 = (f32[4,2,16,384]{3,2,1,0:T(8,128)S(1)}, f32[4,2,16,384]{3,2,1,0:T(8,128)}, u32[]{:S(2)}) copy-start(f32[4,2,16,384]{3,2,1,0:T(8,128)} %refs_10_.1) | copy-start | bytes 589828
  11.0 15.4 %collective-permute-start.1 = (bf16[2,2,16,384]{3,2,1,0:T(8,128)(2,1)S(1)}, bf16[2,2,16,384]{3,2,1,0:T(8,128)(2,1)S(1)}, u32[]{:S(2)}, u32[]{:S(2)}) collective-permute-start(bf16[2,2,16,384]{3,2,1,0:T(8,128)(2,1)S(1)} %shard_map.148), channel_id=1, source_target_pairs={{1,2},{2,1},{3,4},{4,3},{5,6},{6,5},{7,8},{8,7},{9,10},{10,9},{11,... | collective-permute-start | bytes 147464 | tf_op jit(solution)/shard_map/ppermute | solution.py:448
  23.8 11.6 %all-to-all-start.1 = ((bf16[32,8,384]{2,1,0:T(8,128)(2,1)}), bf16[32,8,384]{2,1,0:T(8,128)(2,1)S(1)}, u32[]{:S(2)}, u32[]{:S(2)}) async-start(bf16[32,8,384]{2,1,0:T(8,128)(2,1)} %shard_map.149.refs_12_), calls=%async_computation.1 | async-start | bytes 393216 | tf_op jit(solution)/shard_map/all_to_all | solution.py:495
  26.3 9.1 %copy-start = (bf16[128,256]{1,0:T(8,128)(2,1)S(1)}, bf16[128,256]{1,0:T(8,128)(2,1)}, u32[]{:S(2)}) copy-start(bf16[128,256]{1,0:T(8,128)(2,1)} %constant.8.clone.order_ref) | copy-start | bytes 196612

commit v4 on v3

--- a/solution.py
+++ b/solution.py
@@ -18,7 +18,7 @@
 BUSY = 4 * 10**10
 SHORT = BUSY
 BAND = 64
-EARLY = 2
+EARLY = 3
 
 
 def dot(lhs, rhs):

time: 36.6 us -> 36.6 us (level)
    all_to_all x1, waiting for transfers between devices: 3.71 us -> 3.04 us  [on_device(): lax.all_to_all(blocks, both, split_axis=0, concat_axis=0, tiled=True)]
  transfers between devices with their start and end apart: 4 -> 4, of which waited for: 2 -> 2; matrix products, arithmetic and copies ran while one was open for 0% -> 0% of each run, Pallas kernels for 41% -> 42%
where the time goes in v4:
time: 36.6 us; the launch traced here: 36.3 us
  Pallas kernels  17 us (46%)
  starting transfers between devices  13.5 us (37%)
  waiting for transfers between devices  4.57 us (12%)
  local copies, waits for them, and re-layouts  1.01 us (3%)
    pallas_call x2, Pallas kernels, score(): call(lambda *refs: score_kernel(spots, len(sources), len(ordered), *refs)...  9.84 us
    all_to_all x1, starting transfers between devices, on_device(): lax.all_to_all(blocks, both, split_axis=0, concat_axis=0, tiled=True)  7.15 us
    pallas_call x1, Pallas kernels, on_device(): call(adjoint_kernel, block, [pltpu.VMEM((2 * cols, 2 * cols), BF16), pltp...  5.39 us
    ppermute x2, starting transfers between devices, halo(): return lax.ppermute(slab, both, across if outward else pairs)  3.8 us
    all_to_all x1, waiting for transfers between devices, on_device(): lax.all_to_all(blocks, both, split_axis=0, concat_axis=0, tiled=True)  3.04 us
    all_to_all x1, starting transfers between devices, on_device(): lax.all_to_all(partial, both, split_axis=0, concat_axis=0, tiled=True)  2.52 us
    all_to_all x1, waiting for transfers between devices, on_device(): lax.all_to_all(partial, both, split_axis=0, concat_axis=0, tiled=True)  1.52 us
    unnamed x30, local copies, waits for them, and re-layouts  1.01 us
  transfers between devices with their start and end apart: 4, of which 2 were waited for; matrix products, arithmetic and copies ran while one was open for 0% of the time, Pallas kernels for 42%

profile of v4, /device:TPU:1, one launch (start us, length us, event | category | flops | bytes accessed | tf_op | source)
XLA Modules:
  0.0 36.3 jit_solution(168214659276729275)
XLA Ops:
  0.0 0.9 %copy-done.3 = f32[4,2,16,384]{3,2,1,0:T(8,128)S(1)} copy-done((f32[4,2,16,384]{3,2,1,0:T(8,128)S(1)}, f32[4,2,16,384]{3,2,1,0:T(8,128)}, u32[]{:S(2)}) %copy-start.3) | copy-done | bytes 196632
  0.9 0.8 %shard_map.145.after_ref = bf16[32,8,384]{2,1,0:T(8,128)(2,1)} custom-call(f32[4,2,16,384]{3,2,1,0:T(8,128)S(1)} %copy-done.3), custom_call_target="tpu_custom_call" | custom-call | flops 40000000000 | bytes 1000000 | tf_op jit(solution)/shard_map/pallas_call | solution.py:438
  1.8 0.0 copy-start.9
  1.8 0.0 copy-start.10
  1.8 0.0 copy-start.11
  1.8 0.0 copy-start.12
  1.9 0.1 collective-permute-start
  2.0 7.2 %all-to-all-start = ((bf16[32,8,384]{2,1,0:T(8,128)(2,1)}), bf16[32,8,384]{2,1,0:T(8,128)(2,1)S(1)}, u32[]{:S(2)}, u32[]{:S(2)}) async-start(bf16[32,8,384]{2,1,0:T(8,128)(2,1)} %shard_map.145.after_ref), calls=%async_computation | async-start | bytes 393216 | tf_op jit(solution)/shard_map/all_to_all | solution.py:451
  9.2 0.0 collective-permute-done.refs_1_.refs_2_
  9.2 2.3 %shard_map.147.after_ref.refs_11_ = f32[1,2,16,384]{3,2,1,0:T(8,128)S(1)} custom-call(f32[4,2,16,384]{3,2,1,0:T(8,128)S(1)} %copy-done.4, bf16[2,2,16,384]{3,2,1,0:T(8,128)(2,1)S(1)} %collective-permute-done.refs_1_.refs_2_, bf16[2,2,16,384]{3,2,1,0:T(8,128)(2,1)S(1)} %collective-permute-done.refs_1_.refs_2_, bf16[3,10,3,128]{3,2,1,0:T(4,128)(2,1)S(1)} %bitcast.4, ...), custom_call_target="tpu_custom_call" | custom-call | flops 40000000000 | bytes 2000000 | tf_op jit(solution)/shard_map/pallas_call | solution.py:460
  11.6 0.0 copy-start.1
  11.6 0.0 copy-start.2
  11.6 0.0 copy-start.13
  11.6 0.0 copy-start.14
  11.6 0.0 copy-start.5
  11.7 3.7 %collective-permute-start.1 = (bf16[2,2,16,384]{3,2,1,0:T(8,128)(2,1)S(1)}, bf16[2,2,16,384]{3,2,1,0:T(8,128)(2,1)S(1)}, u32[]{:S(2)}, u32[]{:S(2)}) collective-permute-start(bf16[2,2,16,384]{3,2,1,0:T(8,128)(2,1)S(1)} %shard_map.148), channel_id=1, source_target_pairs={{1,2},{2,1},{3,4},{4,3},{5,6},{6,5},{7,8},{8,7},{9,10},{10,9},{11,... | collective-permute-start | bytes 147464 | tf_op jit(solution)/shard_map/ppermute | solution.py:448
  15.3 3.0 %all-to-all-done.planes_ref = bf16[32,8,384]{2,1,0:T(8,128)(2,1)S(1)} async-done(((bf16[32,8,384]{2,1,0:T(8,128)(2,1)}), bf16[32,8,384]{2,1,0:T(8,128)(2,1)S(1)}, u32[]{:S(2)}, u32[]{:S(2)}) %all-to-all-start) | async-done | bytes 196640 | tf_op jit(solution)/shard_map/all_to_all | solution.py:451
  18.4 5.4 %shard_map.149.refs_12_ = bf16[32,8,384]{2,1,0:T(8,128)(2,1)} custom-call(bf16[32,8,384]{2,1,0:T(8,128)(2,1)S(1)} %all-to-all-done.planes_ref, bf16[8,2,1,384,128]{4,3,2,1,0:T(8,128)(2,1)S(1)} %copy-done.1, bf16[8,2,1,384,128]{4,3,2,1,0:T(8,128)(2,1)} %measured_hbm.1, s32[384,128]{1,0:T(8,128)S(1)} %copy-done.2, bf16[384,768]{1,0:T(8,128)(2,1)S(1)} %copy-done.13, ...), custom_call_target="tpu_custom_call" | custom-call | flops 40000000000 | bytes 5000000 | tf_op jit(solution)/shard_map/pallas_call | solution.py:489
  23.8 2.5 %all-to-all-start.1 = ((bf16[32,8,384]{2,1,0:T(8,128)(2,1)}), bf16[32,8,384]{2,1,0:T(8,128)(2,1)S(1)}, u32[]{:S(2)}, u32[]{:S(2)}) async-start(bf16[32,8,384]{2,1,0:T(8,128)(2,1)} %shard_map.149.refs_12_), calls=%async_computation.1 | async-start | bytes 393216 | tf_op jit(solution)/shard_map/all_to_all | solution.py:495
  26.3 0.0 copy-start
  26.3 0.0 collective-permute-done.1.refs_2_
  26.4 7.5 %shard_map.150.moved_ref = f32[4,2,16,384]{3,2,1,0:T(8,128)S(1)} custom-call(f32[4,2,16,384]{3,2,1,0:T(8,128)S(1)} %copy-done.4, bf16[2,2,16,384]{3,2,1,0:T(8,128)(2,1)S(1)} %collective-permute-done.refs_1_.refs_2_, bf16[2,2,16,384]{3,2,1,0:T(8,128)(2,1)S(1)} %collective-permute-done.1.refs_2_, bf16[3,10,3,128]{3,2,1,0:T(4,128)(2,1)S(1)} %bitcast.5, ...), custom_call_target="tpu_custom_call" | custom-call | flops 40000000000 | bytes 2000000 | tf_op jit(solution)/shard_map/pallas_call | solution.py:460
  33.9 1.5 %all-to-all-done.1.back_ref = bf16[32,8,384]{2,1,0:T(8,128)(2,1)S(1)} async-done(((bf16[32,8,384]{2,1,0:T(8,128)(2,1)}), bf16[32,8,384]{2,1,0:T(8,128)(2,1)S(1)}, u32[]{:S(2)}, u32[]{:S(2)}) %all-to-all-start.1) | async-done | bytes 196640 | tf_op jit(solution)/shard_map/all_to_all | solution.py:495
  35.4 0.9 %shard_map.151 = f32[4,2,16,384]{3,2,1,0:T(8,128)} custom-call(f32[4,2,16,384]{3,2,1,0:T(8,128)S(1)} %shard_map.150.moved_ref, bf16[32,8,384]{2,1,0:T(8,128)(2,1)S(1)} %all-to-all-done.1.back_ref, bf16[128,256]{1,0:T(8,128)(2,1)S(1)} %copy-done), custom_call_target="tpu_custom_call" | custom-call | bytes 1000000 | tf_op jit(solution)/shard_map/pallas_call | solution.py:496
  (21 shorter events, 0.1 us)
Async XLA Ops:
  0.0 0.9 %copy-start.3 = (f32[4,2,16,384]{3,2,1,0:T(8,128)S(1)}, f32[4,2,16,384]{3,2,1,0:T(8,128)}, u32[]{:S(2)}) copy-start(f32[4,2,16,384]{3,2,1,0:T(8,128)} %refs_0_.3) | copy-start | bytes 589828
  1.8 7.4 %copy-start.4 = (f32[4,2,16,384]{3,2,1,0:T(8,128)S(1)}, f32[4,2,16,384]{3,2,1,0:T(8,128)}, u32[]{:S(2)}) copy-start(f32[4,2,16,384]{3,2,1,0:T(8,128)} %refs_0_.3) | copy-start | bytes 589828
  1.8 7.4 %copy-start.6 = (bf16[128,128]{1,0:T(8,128)(2,1)S(1)}, bf16[128,128]{1,0:T(8,128)(2,1)}, u32[]{:S(2)}) copy-start(bf16[128,128]{1,0:T(8,128)(2,1)} %refs_5_.3) | copy-start | bytes 98308
  1.8 7.4 %copy-start.7 = (bf16[128,128]{1,0:T(8,128)(2,1)S(1)}, bf16[128,128]{1,0:T(8,128)(2,1)}, u32[]{:S(2)}) copy-start(bf16[128,128]{1,0:T(8,128)(2,1)} %refs_7_.3) | copy-start | bytes 98308
  1.8 7.4 %copy-start.8 = (bf16[3,3,10,128]{3,1,2,0:T(4,128)(2,1)S(1)}, bf16[3,3,10,128]{3,1,2,0:T(4,128)(2,1)}, u32[]{:S(2)}) copy-start(bf16[3,3,10,128]{3,1,2,0:T(4,128)(2,1)} %param.20) | copy-start | bytes 69124
  1.8 7.4 %copy-start.9 = (bf16[3,3,2,128]{3,2,1,0:T(2,128)(2,1)S(1)}, bf16[3,3,2,128]{3,2,1,0:T(2,128)(2,1)}, u32[]{:S(2)}) copy-start(bf16[3,3,2,128]{3,2,1,0:T(2,128)(2,1)} %refs_9_.3) | copy-start | bytes 13828
  1.8 7.4 %copy-start.10 = (f32[128]{0:T(128)S(1)}, f32[128]{0:T(128)}, u32[]{:S(2)}) copy-start(f32[128]{0:T(128)} %param.21) | copy-start | bytes 1540
  1.8 7.4 %copy-start.11 = (f32[128]{0:T(128)S(1)}, f32[128]{0:T(128)}, u32[]{:S(2)}) copy-start(f32[128]{0:T(128)} %param.23) | copy-start | bytes 1540
  1.8 7.4 %copy-start.12 = (f32[128]{0:T(128)S(1)}, f32[128]{0:T(128)}, u32[]{:S(2)}) copy-start(f32[128]{0:T(128)} %param.25) | copy-start | bytes 1540
  1.9 7.3 %collective-permute-start = (bf16[2,2,16,384]{3,2,1,0:T(8,128)(2,1)S(1)}, bf16[2,2,16,384]{3,2,1,0:T(8,128)(2,1)S(1)}, u32[]{:S(2)}, u32[]{:S(2)}) collective-permute-start(bf16[2,2,16,384]{3,2,1,0:T(8,128)(2,1)S(1)} %shard_map.146), channel_id=1, source_target_pairs={{0,1},{1,0},{2,3},{3,2},{4,5},{5,4},{6,7},{7,6},{8,9},{9,8},{10,11... | collective-permute-start | bytes 147464 | tf_op jit(solution)/shard_map/ppermute | solution.py:448
  2.0 16.4 %all-to-all-start = ((bf16[32,8,384]{2,1,0:T(8,128)(2,1)}), bf16[32,8,384]{2,1,0:T(8,128)(2,1)S(1)}, u32[]{:S(2)}, u32[]{:S(2)}) async-start(bf16[32,8,384]{2,1,0:T(8,128)(2,1)} %shard_map.145.after_ref), calls=%async_computation | async-start | bytes 393216 | tf_op jit(solution)/shard_map/all_to_all | solution.py:451
  11.6 6.8 %copy-start.1 = (bf16[8,2,1,384,128]{4,3,2,1,0:T(8,128)(2,1)S(1)}, bf16[8,2,1,384,128]{4,3,2,1,0:T(8,128)(2,1)}, u32[]{:S(2)}) copy-start(bf16[8,2,1,384,128]{4,3,2,1,0:T(8,128)(2,1)} %sens_ref.1) | copy-start | bytes 4718596
  11.6 6.8 %copy-start.2 = (s32[384,128]{1,0:T(8,128)S(1)}, s32[384,128]{1,0:T(8,128)}, u32[]{:S(2)}) copy-start(s32[384,128]{1,0:T(8,128)} %mask_ref.1) | copy-start | bytes 589828
  11.6 6.8 %copy-start.13 = (bf16[384,768]{1,0:T(8,128)(2,1)S(1)}, bf16[384,768]{1,0:T(8,128)(2,1)}, u32[]{:S(2)}) copy-start(bf16[384,768]{1,0:T(8,128)(2,1)} %constant.6.clone.half_ref) | copy-start | bytes 1769476
  11.6 6.8 %copy-start.14 = (bf16[512,256]{1,0:T(8,128)(2,1)S(1)}, bf16[512,256]{1,0:T(8,128)(2,1)}, u32[]{:S(2)}) copy-start(bf16[512,256]{1,0:T(8,128)(2,1)} %constant.7.clone.z_ref) | copy-start | bytes 786436
  11.6 14.7 %copy-start.5 = (f32[4,2,16,384]{3,2,1,0:T(8,128)S(1)}, f32[4,2,16,384]{3,2,1,0:T(8,128)}, u32[]{:S(2)}) copy-start(f32[4,2,16,384]{3,2,1,0:T(8,128)} %refs_10_.1) | copy-start | bytes 589828
  11.7 14.7 %collective-permute-start.1 = (bf16[2,2,16,384]{3,2,1,0:T(8,128)(2,1)S(1)}, bf16[2,2,16,384]{3,2,1,0:T(8,128)(2,1)S(1)}, u32[]{:S(2)}, u32[]{:S(2)}) collective-permute-start(bf16[2,2,16,384]{3,2,1,0:T(8,128)(2,1)S(1)} %shard_map.148), channel_id=1, source_target_pairs={{1,2},{2,1},{3,4},{4,3},{5,6},{6,5},{7,8},{8,7},{9,10},{10,9},{11,... | collective-permute-start | bytes 147464 | tf_op jit(solution)/shard_map/ppermute | solution.py:448
  23.8 11.6 %all-to-all-start.1 = ((bf16[32,8,384]{2,1,0:T(8,128)(2,1)}), bf16[32,8,384]{2,1,0:T(8,128)(2,1)S(1)}, u32[]{:S(2)}, u32[]{:S(2)}) async-start(bf16[32,8,384]{2,1,0:T(8,128)(2,1)} %shard_map.149.refs_12_), calls=%async_computation.1 | async-start | bytes 393216 | tf_op jit(solution)/shard_map/all_to_all | solution.py:495
  26.3 9.1 %copy-start = (bf16[128,256]{1,0:T(8,128)(2,1)S(1)}, bf16[128,256]{1,0:T(8,128)(2,1)}, u32[]{:S(2)}) copy-start(bf16[128,256]{1,0:T(8,128)(2,1)} %constant.8.clone.order_ref) | copy-start | bytes 196612
